TPU v7x, 512 devices: a whole 4x8x8 slice. The times are simulated.
512 devices in a mesh: row: 64 (over x, z, core), col: 8 (over y).
Axes of the slice: x: 4, y: 8, z: 8, core: 2. Of those that a mesh axis runs over, the one named last changes fastest.
Arguments:
- eig_slab: float32 [32768, 4096], P('row', 'col'), may hold values from -6 to 6
- reflectors: float32 [16, 32768], P('col', 'row'), may hold values from -6 to 6
- row_offsets: int32 [16], replicated, may hold values from 1 to 24, as said below
Outputs:
- rotated: float32 [32768, 4096], P('row', 'col')
Inputs may be any that keep to these rules, and one draw needn't show every extreme that they name: row_offsets[0] is 1; each next one is 1 or 2 larger than the one before, and exactly 8 of these steps are 2.
All inputs are finite; a program needn't handle non-finite values.
Results may differ from a plain program's by a relative error of at most 0.00027.
Values sent between devices are 32-bit elements; how exact they have to be, the bound alone decides.
A program may use at most 64 MiB of HBM per device.

v0:
```python
import jax
import jax.numpy as jnp
from jax import lax
from jax.sharding import PartitionSpec as P

WIDTH = 64
SWEEPS = 16


def extended_2(cells, sides, width):
    for axis, dim in sides:
        count = lax.axis_size(axis)
        ends = count - 1
        head = lax.slice_in_dim(cells, 0, width, axis=dim)
        tail = lax.slice_in_dim(cells, cells.shape[dim] - width, cells.shape[dim], axis=dim)
        cells = jnp.concatenate(
            [
                lax.ppermute(tail, axis, [(i, (i + 1) % count) for i in range(ends)]),
                cells,
                lax.ppermute(head, axis, [((i + 1) % count, i) for i in range(ends)]),
            ],
            axis=dim,
        )
    return cells


def apply_sweep(eig_rows, eigen_columns, first_row, row_displacement, row_count_total, band_width):
    length, columns = eig_rows.shape
    overall_row_span = first_row + jnp.arange(length, dtype=jnp.int32)
    active_flags = (overall_row_span >= row_displacement) & (overall_row_span < row_count_total)
    eigen_columns = jnp.where(active_flags, eigen_columns, jnp.float32(0.0))
    shift = jnp.mod(row_displacement - first_row, band_width)
    zero_rows = jnp.zeros((band_width, columns), eig_rows.dtype)
    padded = jnp.concatenate([zero_rows, eig_rows, zero_rows], axis=0)
    zero_vec = jnp.zeros((band_width,), eigen_columns.dtype)
    padded_vec = jnp.concatenate([zero_vec, eigen_columns, zero_vec])
    integer_nought = jnp.zeros((band_width,), jnp.int32)
    extended_active_flags = jnp.concatenate(
        [integer_nought, active_flags.astype(jnp.int32), integer_nought]
    )
    windows_count = (length + band_width) // band_width
    windows = lax.dynamic_slice_in_dim(padded, shift, length + band_width, 0).reshape(
        windows_count, band_width, columns
    )
    window_vecs = lax.dynamic_slice_in_dim(padded_vec, shift, length + band_width, 0).reshape(
        windows_count, band_width
    )
    live_count = jnp.sum(
        lax.dynamic_slice_in_dim(extended_active_flags, shift, length + band_width, 0).reshape(
            windows_count, band_width
        ),
        axis=1,
    )
    squares = jnp.sum(window_vecs * window_vecs, axis=1)
    factor = jnp.where(
        live_count > 0, 2.0 / (squares + (live_count == 0).astype(jnp.float32)), jnp.float32(0.0)
    )
    project = jnp.einsum("wr,wrc->wc", window_vecs, windows, precision=lax.Precision.HIGHEST)
    updated = windows - (factor[:, None] * window_vecs)[:, :, None] * project[:, None, :]
    padded = lax.dynamic_update_slice_in_dim(
        padded, updated.reshape(length + band_width, columns), shift, 0
    )
    return padded[band_width : band_width + length]


def local(eig_slab, reflectors, row_offsets):
    local_rows = eig_slab.shape[0]
    row_count_total = local_rows * lax.axis_size("row")
    depth = 1
    margin = depth * WIDTH
    base_row = lax.axis_index("row") * local_rows
    first_row = base_row - margin
    vec_rims = extended_2(reflectors, (("row", 1),), margin)
    all_vectors = lax.all_gather(vec_rims, "col", axis=0, tiled=True)

    def one_round(round_index, current):
        extended = extended_2(current, (("row", 0),), margin)
        sweep_index = round_index * depth + 0
        eigen_columns = lax.dynamic_index_in_dim(all_vectors, sweep_index, 0, keepdims=False)
        row_displacement = lax.dynamic_index_in_dim(row_offsets, sweep_index, 0, keepdims=False)
        extended = apply_sweep(
            extended, eigen_columns, first_row, row_displacement, row_count_total, WIDTH
        )
        return extended[margin : margin + local_rows]

    return lax.fori_loop(0, SWEEPS // depth, one_round, eig_slab)


def solution(mesh):
    placed = (P("row", "col"), P("col", "row"), P())
    return jax.shard_map(
        local, mesh=mesh, in_specs=placed, out_specs=P("row", "col"), check_vma=False
    )
```

profile of v0, /device:TPU:6, one launch (start us, length us, event | category | flops | bytes accessed | tf_op | source)
XLA Modules:
  0.0 266.7 jit_solution(5024641922731427094)
XLA Ops:
  2.8 10.7 %collective-permute-start.3 = (f32[2,64]{1,0:T(2,128)S(1)}, f32[2,64]{1,0:T(2,128)S(1)}, u32[]{:S(2)}, u32[]{:S(2)}) collective-permute-start(f32[2,64]{1,0:T(2,128)S(1)} %get-tuple-element.152), channel_id=1, source_target_pairs={{8,0},{16,8},{24,16},{32,24},{40,32},{48,40},{56,48},{64,56},{72,6... | collective-permute-start | bytes 1544 | tf_op jit(solution)/shard_map/ppermute | solution.py:20
  14.8 26.2 %all-gather = f32[8,2,640]{2,1,0:T(2,128)S(1)} all-gather(f32[1,2,640]{2,1,0:T(2,128)S(1)} %maximum_bitcast_fusion), channel_id=1, replica_groups=mesh['row'=64,'col'=8] {'col'}, dimensions={0}, use_global_device_ids=true | all-gather | bytes 46080 | tf_op jit(solution)/shard_map/all_gather | solution.py:74
  41.0 224.7 %while.15 = (s32[]{:T(128)}, f32[512,512]{1,0:T(8,128)S(1)}, s32[16]{0:T(128)S(1)}, s32[]{:T(128)}, f32[16,640]{1,0:T(8,128)S(1)}, /*index=5*/s32[]{:T(128)}, f3...) while((s32[]{:T(128)}, f32[512,512]{1,0:T(8,128)S(1)}, s32[16]{0:T(128)S(1)}, s32[]{:T(128)}, ...), condition=%wide.region_3.4_spmd, body=%wide.region_0.3_spmd.sunk | while | flops 5058621 | bytes 16818340 | solution.py:86
  41.1 1.9 collective-permute-start
  43.0 5.8 %collective-permute-start.1 = (f32[64,512]{1,0:T(8,128)S(1)}, f32[64,512]{1,0:T(8,128)S(1)}, u32[]{:S(2)}, u32[]{:S(2)}) collective-permute-start(f32[64,512]{1,0:T(8,128)S(1)} %get-tuple-element.187), channel_id=1, source_target_pairs={{8,0},{16,8},{24,16},{32,24},{40,32},{48,40},{56,48},{64,56},{72,6... | collective-permute-start | bytes 393224 | tf_op jit(solution)/shard_map/while/body/eval_jaxpr/ppermute | solution.py:20
  55.0 1.9 collective-permute-start
  57.0 5.8 %collective-permute-start.1 = (f32[64,512]{1,0:T(8,128)S(1)}, f32[64,512]{1,0:T(8,128)S(1)}, u32[]{:S(2)}, u32[]{:S(2)}) collective-permute-start(f32[64,512]{1,0:T(8,128)S(1)} %get-tuple-element.187), channel_id=1, source_target_pairs={{8,0},{16,8},{24,16},{32,24},{40,32},{48,40},{56,48},{64,56},{72,6... | collective-permute-start | bytes 393224 | tf_op jit(solution)/shard_map/while/body/eval_jaxpr/ppermute | solution.py:20
  70.9 5.8 %collective-permute-start.1 = (f32[64,512]{1,0:T(8,128)S(1)}, f32[64,512]{1,0:T(8,128)S(1)}, u32[]{:S(2)}, u32[]{:S(2)}) collective-permute-start(f32[64,512]{1,0:T(8,128)S(1)} %get-tuple-element.187), channel_id=1, source_target_pairs={{8,0},{16,8},{24,16},{32,24},{40,32},{48,40},{56,48},{64,56},{72,6... | collective-permute-start | bytes 393224 | tf_op jit(solution)/shard_map/while/body/eval_jaxpr/ppermute | solution.py:20
  84.9 5.8 %collective-permute-start.1 = (f32[64,512]{1,0:T(8,128)S(1)}, f32[64,512]{1,0:T(8,128)S(1)}, u32[]{:S(2)}, u32[]{:S(2)}) collective-permute-start(f32[64,512]{1,0:T(8,128)S(1)} %get-tuple-element.187), channel_id=1, source_target_pairs={{8,0},{16,8},{24,16},{32,24},{40,32},{48,40},{56,48},{64,56},{72,6... | collective-permute-start | bytes 393224 | tf_op jit(solution)/shard_map/while/body/eval_jaxpr/ppermute | solution.py:20
  98.8 5.8 %collective-permute-start.1 = (f32[64,512]{1,0:T(8,128)S(1)}, f32[64,512]{1,0:T(8,128)S(1)}, u32[]{:S(2)}, u32[]{:S(2)}) collective-permute-start(f32[64,512]{1,0:T(8,128)S(1)} %get-tuple-element.187), channel_id=1, source_target_pairs={{8,0},{16,8},{24,16},{32,24},{40,32},{48,40},{56,48},{64,56},{72,6... | collective-permute-start | bytes 393224 | tf_op jit(solution)/shard_map/while/body/eval_jaxpr/ppermute | solution.py:20
  110.8 1.9 collective-permute-start
  112.8 5.8 %collective-permute-start.1 = (f32[64,512]{1,0:T(8,128)S(1)}, f32[64,512]{1,0:T(8,128)S(1)}, u32[]{:S(2)}, u32[]{:S(2)}) collective-permute-start(f32[64,512]{1,0:T(8,128)S(1)} %get-tuple-element.187), channel_id=1, source_target_pairs={{8,0},{16,8},{24,16},{32,24},{40,32},{48,40},{56,48},{64,56},{72,6... | collective-permute-start | bytes 393224 | tf_op jit(solution)/shard_map/while/body/eval_jaxpr/ppermute | solution.py:20
  126.8 5.8 %collective-permute-start.1 = (f32[64,512]{1,0:T(8,128)S(1)}, f32[64,512]{1,0:T(8,128)S(1)}, u32[]{:S(2)}, u32[]{:S(2)}) collective-permute-start(f32[64,512]{1,0:T(8,128)S(1)} %get-tuple-element.187), channel_id=1, source_target_pairs={{8,0},{16,8},{24,16},{32,24},{40,32},{48,40},{56,48},{64,56},{72,6... | collective-permute-start | bytes 393224 | tf_op jit(solution)/shard_map/while/body/eval_jaxpr/ppermute | solution.py:20
  140.9 5.8 %collective-permute-start.1 = (f32[64,512]{1,0:T(8,128)S(1)}, f32[64,512]{1,0:T(8,128)S(1)}, u32[]{:S(2)}, u32[]{:S(2)}) collective-permute-start(f32[64,512]{1,0:T(8,128)S(1)} %get-tuple-element.187), channel_id=1, source_target_pairs={{8,0},{16,8},{24,16},{32,24},{40,32},{48,40},{56,48},{64,56},{72,6... | collective-permute-start | bytes 393224 | tf_op jit(solution)/shard_map/while/body/eval_jaxpr/ppermute | solution.py:20
  153.1 1.9 collective-permute-start
  155.0 5.8 %collective-permute-start.1 = (f32[64,512]{1,0:T(8,128)S(1)}, f32[64,512]{1,0:T(8,128)S(1)}, u32[]{:S(2)}, u32[]{:S(2)}) collective-permute-start(f32[64,512]{1,0:T(8,128)S(1)} %get-tuple-element.187), channel_id=1, source_target_pairs={{8,0},{16,8},{24,16},{32,24},{40,32},{48,40},{56,48},{64,56},{72,6... | collective-permute-start | bytes 393224 | tf_op jit(solution)/shard_map/while/body/eval_jaxpr/ppermute | solution.py:20
  169.1 5.8 %collective-permute-start.1 = (f32[64,512]{1,0:T(8,128)S(1)}, f32[64,512]{1,0:T(8,128)S(1)}, u32[]{:S(2)}, u32[]{:S(2)}) collective-permute-start(f32[64,512]{1,0:T(8,128)S(1)} %get-tuple-element.187), channel_id=1, source_target_pairs={{8,0},{16,8},{24,16},{32,24},{40,32},{48,40},{56,48},{64,56},{72,6... | collective-permute-start | bytes 393224 | tf_op jit(solution)/shard_map/while/body/eval_jaxpr/ppermute | solution.py:20
  183.2 5.8 %collective-permute-start.1 = (f32[64,512]{1,0:T(8,128)S(1)}, f32[64,512]{1,0:T(8,128)S(1)}, u32[]{:S(2)}, u32[]{:S(2)}) collective-permute-start(f32[64,512]{1,0:T(8,128)S(1)} %get-tuple-element.187), channel_id=1, source_target_pairs={{8,0},{16,8},{24,16},{32,24},{40,32},{48,40},{56,48},{64,56},{72,6... | collective-permute-start | bytes 393224 | tf_op jit(solution)/shard_map/while/body/eval_jaxpr/ppermute | solution.py:20
  197.3 5.8 %collective-permute-start.1 = (f32[64,512]{1,0:T(8,128)S(1)}, f32[64,512]{1,0:T(8,128)S(1)}, u32[]{:S(2)}, u32[]{:S(2)}) collective-permute-start(f32[64,512]{1,0:T(8,128)S(1)} %get-tuple-element.187), channel_id=1, source_target_pairs={{8,0},{16,8},{24,16},{32,24},{40,32},{48,40},{56,48},{64,56},{72,6... | collective-permute-start | bytes 393224 | tf_op jit(solution)/shard_map/while/body/eval_jaxpr/ppermute | solution.py:20
  209.5 1.9 collective-permute-start
  211.4 5.8 %collective-permute-start.1 = (f32[64,512]{1,0:T(8,128)S(1)}, f32[64,512]{1,0:T(8,128)S(1)}, u32[]{:S(2)}, u32[]{:S(2)}) collective-permute-start(f32[64,512]{1,0:T(8,128)S(1)} %get-tuple-element.187), channel_id=1, source_target_pairs={{8,0},{16,8},{24,16},{32,24},{40,32},{48,40},{56,48},{64,56},{72,6... | collective-permute-start | bytes 393224 | tf_op jit(solution)/shard_map/while/body/eval_jaxpr/ppermute | solution.py:20
  225.5 5.8 %collective-permute-start.1 = (f32[64,512]{1,0:T(8,128)S(1)}, f32[64,512]{1,0:T(8,128)S(1)}, u32[]{:S(2)}, u32[]{:S(2)}) collective-permute-start(f32[64,512]{1,0:T(8,128)S(1)} %get-tuple-element.187), channel_id=1, source_target_pairs={{8,0},{16,8},{24,16},{32,24},{40,32},{48,40},{56,48},{64,56},{72,6... | collective-permute-start | bytes 393224 | tf_op jit(solution)/shard_map/while/body/eval_jaxpr/ppermute | solution.py:20
  239.6 5.8 %collective-permute-start.1 = (f32[64,512]{1,0:T(8,128)S(1)}, f32[64,512]{1,0:T(8,128)S(1)}, u32[]{:S(2)}, u32[]{:S(2)}) collective-permute-start(f32[64,512]{1,0:T(8,128)S(1)} %get-tuple-element.187), channel_id=1, source_target_pairs={{8,0},{16,8},{24,16},{32,24},{40,32},{48,40},{56,48},{64,56},{72,6... | collective-permute-start | bytes 393224 | tf_op jit(solution)/shard_map/while/body/eval_jaxpr/ppermute | solution.py:20
  253.7 5.8 %collective-permute-start.1 = (f32[64,512]{1,0:T(8,128)S(1)}, f32[64,512]{1,0:T(8,128)S(1)}, u32[]{:S(2)}, u32[]{:S(2)}) collective-permute-start(f32[64,512]{1,0:T(8,128)S(1)} %get-tuple-element.187), channel_id=1, source_target_pairs={{8,0},{16,8},{24,16},{32,24},{40,32},{48,40},{56,48},{64,56},{72,6... | collective-permute-start | bytes 393224 | tf_op jit(solution)/shard_map/while/body/eval_jaxpr/ppermute | solution.py:20
  (553 shorter events, 114.9 us)
Async XLA Ops:
  0.9 12.6 %collective-permute-start.2 = (f32[2,64]{1,0:T(2,128)S(1)}, f32[2,64]{1,0:T(2,128)S(1)}, u32[]{:S(2)}, u32[]{:S(2)}) collective-permute-start(f32[2,64]{1,0:T(2,128)S(1)} %get-tuple-element.151), channel_id=1, source_target_pairs={{0,8},{8,16},{16,24},{24,32},{32,40},{40,48},{48,56},{56,64},{64,7... | collective-permute-start | bytes 1544 | tf_op jit(solution)/shard_map/ppermute | solution.py:18
  2.8 11.9 %collective-permute-start.3 = (f32[2,64]{1,0:T(2,128)S(1)}, f32[2,64]{1,0:T(2,128)S(1)}, u32[]{:S(2)}, u32[]{:S(2)}) collective-permute-start(f32[2,64]{1,0:T(2,128)S(1)} %get-tuple-element.152), channel_id=1, source_target_pairs={{8,0},{16,8},{24,16},{32,24},{40,32},{48,40},{56,48},{64,56},{72,6... | collective-permute-start | bytes 1544 | tf_op jit(solution)/shard_map/ppermute | solution.py:20
  41.1 11.3 %collective-permute-start = (f32[64,512]{1,0:T(8,128)S(1)}, f32[64,512]{1,0:T(8,128)S(1)}, u32[]{:S(2)}, u32[]{:S(2)}) collective-permute-start(f32[64,512]{1,0:T(8,128)S(1)} %get-tuple-element.186), channel_id=1, source_target_pairs={{0,8},{8,16},{16,24},{24,32},{32,40},{40,48},{48,56},{56,64},{64,7... | collective-permute-start | bytes 393224 | tf_op jit(solution)/shard_map/while/body/eval_jaxpr/ppermute | solution.py:18
  43.0 9.4 %collective-permute-start.1 = (f32[64,512]{1,0:T(8,128)S(1)}, f32[64,512]{1,0:T(8,128)S(1)}, u32[]{:S(2)}, u32[]{:S(2)}) collective-permute-start(f32[64,512]{1,0:T(8,128)S(1)} %get-tuple-element.187), channel_id=1, source_target_pairs={{8,0},{16,8},{24,16},{32,24},{40,32},{48,40},{56,48},{64,56},{72,6... | collective-permute-start | bytes 393224 | tf_op jit(solution)/shard_map/while/body/eval_jaxpr/ppermute | solution.py:20
  55.0 11.3 %collective-permute-start = (f32[64,512]{1,0:T(8,128)S(1)}, f32[64,512]{1,0:T(8,128)S(1)}, u32[]{:S(2)}, u32[]{:S(2)}) collective-permute-start(f32[64,512]{1,0:T(8,128)S(1)} %get-tuple-element.186), channel_id=1, source_target_pairs={{0,8},{8,16},{16,24},{24,32},{32,40},{40,48},{48,56},{56,64},{64,7... | collective-permute-start | bytes 393224 | tf_op jit(solution)/shard_map/while/body/eval_jaxpr/ppermute | solution.py:18
  69.0 11.3 %collective-permute-start = (f32[64,512]{1,0:T(8,128)S(1)}, f32[64,512]{1,0:T(8,128)S(1)}, u32[]{:S(2)}, u32[]{:S(2)}) collective-permute-start(f32[64,512]{1,0:T(8,128)S(1)} %get-tuple-element.186), channel_id=1, source_target_pairs={{0,8},{8,16},{16,24},{24,32},{32,40},{40,48},{48,56},{56,64},{64,7... | collective-permute-start | bytes 393224 | tf_op jit(solution)/shard_map/while/body/eval_jaxpr/ppermute | solution.py:18
  82.9 11.3 %collective-permute-start = (f32[64,512]{1,0:T(8,128)S(1)}, f32[64,512]{1,0:T(8,128)S(1)}, u32[]{:S(2)}, u32[]{:S(2)}) collective-permute-start(f32[64,512]{1,0:T(8,128)S(1)} %get-tuple-element.186), channel_id=1, source_target_pairs={{0,8},{8,16},{16,24},{24,32},{32,40},{40,48},{48,56},{56,64},{64,7... | collective-permute-start | bytes 393224 | tf_op jit(solution)/shard_map/while/body/eval_jaxpr/ppermute | solution.py:18
  84.9 9.4 %collective-permute-start.1 = (f32[64,512]{1,0:T(8,128)S(1)}, f32[64,512]{1,0:T(8,128)S(1)}, u32[]{:S(2)}, u32[]{:S(2)}) collective-permute-start(f32[64,512]{1,0:T(8,128)S(1)} %get-tuple-element.187), channel_id=1, source_target_pairs={{8,0},{16,8},{24,16},{32,24},{40,32},{48,40},{56,48},{64,56},{72,6... | collective-permute-start | bytes 393224 | tf_op jit(solution)/shard_map/while/body/eval_jaxpr/ppermute | solution.py:20
  96.9 11.3 %collective-permute-start = (f32[64,512]{1,0:T(8,128)S(1)}, f32[64,512]{1,0:T(8,128)S(1)}, u32[]{:S(2)}, u32[]{:S(2)}) collective-permute-start(f32[64,512]{1,0:T(8,128)S(1)} %get-tuple-element.186), channel_id=1, source_target_pairs={{0,8},{8,16},{16,24},{24,32},{32,40},{40,48},{48,56},{56,64},{64,7... | collective-permute-start | bytes 393224 | tf_op jit(solution)/shard_map/while/body/eval_jaxpr/ppermute | solution.py:18
  110.8 11.3 %collective-permute-start = (f32[64,512]{1,0:T(8,128)S(1)}, f32[64,512]{1,0:T(8,128)S(1)}, u32[]{:S(2)}, u32[]{:S(2)}) collective-permute-start(f32[64,512]{1,0:T(8,128)S(1)} %get-tuple-element.186), channel_id=1, source_target_pairs={{0,8},{8,16},{16,24},{24,32},{32,40},{40,48},{48,56},{56,64},{64,7... | collective-permute-start | bytes 393224 | tf_op jit(solution)/shard_map/while/body/eval_jaxpr/ppermute | solution.py:18
  112.8 9.4 %collective-permute-start.1 = (f32[64,512]{1,0:T(8,128)S(1)}, f32[64,512]{1,0:T(8,128)S(1)}, u32[]{:S(2)}, u32[]{:S(2)}) collective-permute-start(f32[64,512]{1,0:T(8,128)S(1)} %get-tuple-element.187), channel_id=1, source_target_pairs={{8,0},{16,8},{24,16},{32,24},{40,32},{48,40},{56,48},{64,56},{72,6... | collective-permute-start | bytes 393224 | tf_op jit(solution)/shard_map/while/body/eval_jaxpr/ppermute | solution.py:20
  124.9 11.3 %collective-permute-start = (f32[64,512]{1,0:T(8,128)S(1)}, f32[64,512]{1,0:T(8,128)S(1)}, u32[]{:S(2)}, u32[]{:S(2)}) collective-permute-start(f32[64,512]{1,0:T(8,128)S(1)} %get-tuple-element.186), channel_id=1, source_target_pairs={{0,8},{8,16},{16,24},{24,32},{32,40},{40,48},{48,56},{56,64},{64,7... | collective-permute-start | bytes 393224 | tf_op jit(solution)/shard_map/while/body/eval_jaxpr/ppermute | solution.py:18
  139.0 11.3 %collective-permute-start = (f32[64,512]{1,0:T(8,128)S(1)}, f32[64,512]{1,0:T(8,128)S(1)}, u32[]{:S(2)}, u32[]{:S(2)}) collective-permute-start(f32[64,512]{1,0:T(8,128)S(1)} %get-tuple-element.186), channel_id=1, source_target_pairs={{0,8},{8,16},{16,24},{24,32},{32,40},{40,48},{48,56},{56,64},{64,7... | collective-permute-start | bytes 393224 | tf_op jit(solution)/shard_map/while/body/eval_jaxpr/ppermute | solution.py:18
  153.1 11.3 %collective-permute-start = (f32[64,512]{1,0:T(8,128)S(1)}, f32[64,512]{1,0:T(8,128)S(1)}, u32[]{:S(2)}, u32[]{:S(2)}) collective-permute-start(f32[64,512]{1,0:T(8,128)S(1)} %get-tuple-element.186), channel_id=1, source_target_pairs={{0,8},{8,16},{16,24},{24,32},{32,40},{40,48},{48,56},{56,64},{64,7... | collective-permute-start | bytes 393224 | tf_op jit(solution)/shard_map/while/body/eval_jaxpr/ppermute | solution.py:18
  155.0 9.4 %collective-permute-start.1 = (f32[64,512]{1,0:T(8,128)S(1)}, f32[64,512]{1,0:T(8,128)S(1)}, u32[]{:S(2)}, u32[]{:S(2)}) collective-permute-start(f32[64,512]{1,0:T(8,128)S(1)} %get-tuple-element.187), channel_id=1, source_target_pairs={{8,0},{16,8},{24,16},{32,24},{40,32},{48,40},{56,48},{64,56},{72,6... | collective-permute-start | bytes 393224 | tf_op jit(solution)/shard_map/while/body/eval_jaxpr/ppermute | solution.py:20
  167.2 11.3 %collective-permute-start = (f32[64,512]{1,0:T(8,128)S(1)}, f32[64,512]{1,0:T(8,128)S(1)}, u32[]{:S(2)}, u32[]{:S(2)}) collective-permute-start(f32[64,512]{1,0:T(8,128)S(1)} %get-tuple-element.186), channel_id=1, source_target_pairs={{0,8},{8,16},{16,24},{24,32},{32,40},{40,48},{48,56},{56,64},{64,7... | collective-permute-start | bytes 393224 | tf_op jit(solution)/shard_map/while/body/eval_jaxpr/ppermute | solution.py:18
  181.3 11.3 %collective-permute-start = (f32[64,512]{1,0:T(8,128)S(1)}, f32[64,512]{1,0:T(8,128)S(1)}, u32[]{:S(2)}, u32[]{:S(2)}) collective-permute-start(f32[64,512]{1,0:T(8,128)S(1)} %get-tuple-element.186), channel_id=1, source_target_pairs={{0,8},{8,16},{16,24},{24,32},{32,40},{40,48},{48,56},{56,64},{64,7... | collective-permute-start | bytes 393224 | tf_op jit(solution)/shard_map/while/body/eval_jaxpr/ppermute | solution.py:18
  195.4 11.3 %collective-permute-start = (f32[64,512]{1,0:T(8,128)S(1)}, f32[64,512]{1,0:T(8,128)S(1)}, u32[]{:S(2)}, u32[]{:S(2)}) collective-permute-start(f32[64,512]{1,0:T(8,128)S(1)} %get-tuple-element.186), channel_id=1, source_target_pairs={{0,8},{8,16},{16,24},{24,32},{32,40},{40,48},{48,56},{56,64},{64,7... | collective-permute-start | bytes 393224 | tf_op jit(solution)/shard_map/while/body/eval_jaxpr/ppermute | solution.py:18
  209.5 11.3 %collective-permute-start = (f32[64,512]{1,0:T(8,128)S(1)}, f32[64,512]{1,0:T(8,128)S(1)}, u32[]{:S(2)}, u32[]{:S(2)}) collective-permute-start(f32[64,512]{1,0:T(8,128)S(1)} %get-tuple-element.186), channel_id=1, source_target_pairs={{0,8},{8,16},{16,24},{24,32},{32,40},{40,48},{48,56},{56,64},{64,7... | collective-permute-start | bytes 393224 | tf_op jit(solution)/shard_map/while/body/eval_jaxpr/ppermute | solution.py:18
  211.4 9.4 %collective-permute-start.1 = (f32[64,512]{1,0:T(8,128)S(1)}, f32[64,512]{1,0:T(8,128)S(1)}, u32[]{:S(2)}, u32[]{:S(2)}) collective-permute-start(f32[64,512]{1,0:T(8,128)S(1)} %get-tuple-element.187), channel_id=1, source_target_pairs={{8,0},{16,8},{24,16},{32,24},{40,32},{48,40},{56,48},{64,56},{72,6... | collective-permute-start | bytes 393224 | tf_op jit(solution)/shard_map/while/body/eval_jaxpr/ppermute | solution.py:20
  223.6 11.3 %collective-permute-start = (f32[64,512]{1,0:T(8,128)S(1)}, f32[64,512]{1,0:T(8,128)S(1)}, u32[]{:S(2)}, u32[]{:S(2)}) collective-permute-start(f32[64,512]{1,0:T(8,128)S(1)} %get-tuple-element.186), channel_id=1, source_target_pairs={{0,8},{8,16},{16,24},{24,32},{32,40},{40,48},{48,56},{56,64},{64,7... | collective-permute-start | bytes 393224 | tf_op jit(solution)/shard_map/while/body/eval_jaxpr/ppermute | solution.py:18
  237.6 11.3 %collective-permute-start = (f32[64,512]{1,0:T(8,128)S(1)}, f32[64,512]{1,0:T(8,128)S(1)}, u32[]{:S(2)}, u32[]{:S(2)}) collective-permute-start(f32[64,512]{1,0:T(8,128)S(1)} %get-tuple-element.186), channel_id=1, source_target_pairs={{0,8},{8,16},{16,24},{24,32},{32,40},{40,48},{48,56},{56,64},{64,7... | collective-permute-start | bytes 393224 | tf_op jit(solution)/shard_map/while/body/eval_jaxpr/ppermute | solution.py:18
  251.7 11.3 %collective-permute-start = (f32[64,512]{1,0:T(8,128)S(1)}, f32[64,512]{1,0:T(8,128)S(1)}, u32[]{:S(2)}, u32[]{:S(2)}) collective-permute-start(f32[64,512]{1,0:T(8,128)S(1)} %get-tuple-element.186), channel_id=1, source_target_pairs={{0,8},{8,16},{16,24},{24,32},{32,40},{40,48},{48,56},{56,64},{64,7... | collective-permute-start | bytes 393224 | tf_op jit(solution)/shard_map/while/body/eval_jaxpr/ppermute | solution.py:18
  253.7 9.4 %collective-permute-start.1 = (f32[64,512]{1,0:T(8,128)S(1)}, f32[64,512]{1,0:T(8,128)S(1)}, u32[]{:S(2)}, u32[]{:S(2)}) collective-permute-start(f32[64,512]{1,0:T(8,128)S(1)} %get-tuple-element.187), channel_id=1, source_target_pairs={{8,0},{16,8},{24,16},{32,24},{40,32},{48,40},{56,48},{64,56},{72,6... | collective-permute-start | bytes 393224 | tf_op jit(solution)/shard_map/while/body/eval_jaxpr/ppermute | solution.py:20
  (14 other events, 178.2 us)
where the time goes:
time: 268 us; the launch traced here: 267 us
  starting transfers between devices  135 us (50%)
  local copies, waits for them, and re-layouts  47 us (18%)
  other arithmetic  31 us (12%)
  blocking collectives  26.2 us (10%)
  loops' own time  13.2 us (5%)
  matrix products  12.6 us (5%)
    ppermute x17, starting transfers between devices, extended_2(): lax.ppermute(head, axis, [((i + 1) % count, i) for i in range(ends)])  103 us
    ppermute x17, starting transfers between devices, extended_2(): lax.ppermute(tail, axis, [(i, (i + 1) % count) for i in range(ends)])  32.6 us
    all_gather x1, blocking collectives, local(): all_vectors = lax.all_gather(vec_rims, 'col', axis=0, tiled=True)  26.2 us
    dynamic_update_slice x16, local copies, waits for them, and re-layouts, apply_sweep(): lax.dynamic_update_slice_in_dim(padded, updated.reshape(length + band_wid...  20.2 us
    another operation x1, loops' own time, local(): return lax.fori_loop(0, SWEEPS // depth, one_round, eig_slab)  13.2 us
    dot_general x16, matrix products, apply_sweep(): jnp.einsum('wr,wrc->wc', window_vecs, windows, precision=lax.Precision.HI...  12.6 us
    dynamic_slice x16, local copies, waits for them, and re-layouts, one_round(): lax.dynamic_index_in_dim(row_offsets, sweep_index, 0, keepdims=False)  9.91 us
    select_n x16, other arithmetic, apply_sweep(): eigen_columns = jnp.where(active_flags, eigen_columns, jnp.float32(0.0))  9.78 us
  transfers between devices with their start and end apart: 34, of which 1 were waited for; matrix products, arithmetic and copies ran while one was open for 18% of the time, Pallas kernels for 0%

commit v1 on v0

v1 whole, which is shorter than its diff:
```python
import functools

import jax
import jax.numpy as jnp
from jax import lax
from jax.experimental import pallas as pl
from jax.experimental.pallas import tpu as pltpu
from jax.sharding import PartitionSpec as P

WIDTH = 64
SWEEPS = 16
RIM = 24
FRAME = WIDTH + RIM
EARLY = 16
LANES = 128
MESH = pl.DeviceIdType.MESH
HIGH = lax.Precision.HIGH
HIGHEST = lax.Precision.HIGHEST


def local_kernel(
    row_count, col_count,
    off_ref, refl_ref, x_ref,
    y_ref, inflow_ref,
    xe, vrec, vv, osend, orec, o2rec,
    x_sem, y_sem, send_sems, recv_sems, edge_send, edge_recv,
):
    per, rows = refl_ref.shape
    cols = x_ref.shape[1]
    wide = cols + LANES
    b = lax.axis_index("row")
    c = lax.axis_index("col")

    def row_at(d):
        return lax.rem(b + d + row_count, row_count)

    def col_at(d):
        return lax.rem(c + d, col_count)

    x_copy = pltpu.make_async_copy(x_ref, xe.at[WIDTH : WIDTH + rows, 0:cols], x_sem)
    x_copy.start()

    barrier = pltpu.get_barrier_semaphore()
    peers = [(b, col_at(d)) for d in range(1, col_count)]
    peers += [(row_at(e), col_at(d)) for e in (1, -1) for d in range(col_count)]
    peers += [(row_at(2), c), (row_at(-2), c)]
    for peer in peers:
        pl.semaphore_signal(barrier, inc=1, device_id=peer, device_id_type=MESH)

    xe[WIDTH + rows : WIDTH + rows + RIM, 0:cols] = jnp.zeros((RIM, cols), jnp.float32)
    xe[0 : WIDTH + rows, cols:wide] = jnp.zeros((WIDTH + rows, LANES), jnp.float32)
    unit = lax.broadcasted_iota(jnp.int32, (RIM, LANES), 0) == lax.broadcasted_iota(
        jnp.int32, (RIM, LANES), 1
    )
    xe[WIDTH + rows : WIDTH + rows + RIM, cols:wide] = jnp.where(unit, 1.0, 0.0)
    vrec[c, :, LANES : LANES + rows] = refl_ref[...]

    pl.semaphore_wait(barrier, len(peers))

    copies = []

    def send(src, dst, slot, sender, peer):
        copy = pltpu.make_async_remote_copy(
            src_ref=src, dst_ref=dst, send_sem=send_sems.at[slot], recv_sem=recv_sems.at[sender],
            device_id=peer, device_id_type=MESH,
        )
        copy.start()
        copies.append(copy)

    slot = 0
    for d in range(1, col_count):
        send(refl_ref, vrec.at[c, :, LANES : LANES + rows], slot, d, (b, col_at(d)))
        slot += 1
    for d in range(col_count):
        send(
            refl_ref.at[:, 0:LANES], vrec.at[c, :, LANES + rows : 2 * LANES + rows],
            slot, col_count + d, (row_at(-1), col_at(d)),
        )
        slot += 1
        send(
            refl_ref.at[:, rows - LANES : rows], vrec.at[c, :, 0:LANES],
            slot, 2 * col_count + d, (row_at(1), col_at(d)),
        )
        slot += 1
    halo = pltpu.make_async_remote_copy(
        src_ref=x_ref.at[rows - WIDTH : rows, :], dst_ref=xe.at[0:WIDTH, 0:cols],
        send_sem=edge_send.at[0], recv_sem=edge_recv.at[0],
        device_id=(row_at(1), c), device_id_type=MESH,
    )
    halo.start()

    for copy in copies:
        copy.wait_recv()

    for i in range(col_count):
        vv[i * per : (i + 1) * per, :] = vrec[i]

    sweep_of = lax.broadcasted_iota(jnp.int32, (SWEEPS, LANES), 0)
    lane_of = lax.broadcasted_iota(jnp.int32, (SWEEPS, LANES), 1)
    first = jnp.zeros((SWEEPS, LANES), jnp.int32)
    for s in range(SWEEPS):
        first = jnp.where(sweep_of == s, off_ref[s], first)
    window = (lane_of >= first) & (lane_of < first + WIDTH)

    vall = vv[...]
    turned = pltpu.roll(vall, vall.shape[1] - WIDTH, 1)
    count = rows // WIDTH + 1
    products = []
    for f in range(count):
        if f % 2 == 0:
            v = turned[:, WIDTH * f : WIDTH * f + LANES]
        else:
            v = vall[:, WIDTH * (f + 1) : WIDTH * (f + 1) + LANES]
        live = window
        if f == 0:
            live = live & (b > 0)
        if f == count - 1:
            live = live & ((lane_of < WIDTH) | (b < row_count - 1))
        v = jnp.where(live, v, 0.0)
        squares = jnp.sum(v * v, axis=1, keepdims=True)
        if f == 0:
            dead = (b == 0).astype(jnp.float32)
            tau = jnp.where(b > 0, 2.0 / (squares + dead), 0.0)
        else:
            tau = 2.0 / squares
        gram = lax.dot_general(
            v, v, (((1,), (1,)), ((), ())), precision=HIGHEST, preferred_element_type=jnp.float32
        )
        below = lax.broadcasted_iota(jnp.int32, (SWEEPS, SWEEPS), 0) > lax.broadcasted_iota(
            jnp.int32, (SWEEPS, SWEEPS), 1
        )
        scaled = jnp.where(below, gram * tau, 0.0)
        w = v * tau
        for j in range(SWEEPS - 1):
            w = w - scaled[:, j : j + 1] * w[j : j + 1, :]
        products.append(
            lax.dot_general(
                v, w, (((0,), (0,)), ((), ())), precision=HIGHEST, preferred_element_type=jnp.float32
            )
        )

    x_copy.wait()
    for f in range(count - 1, -1, -1):
        if f == 0:
            osend[...] = xe[WIDTH : WIDTH + RIM, :]
            far = pltpu.make_async_remote_copy(
                src_ref=osend.at[0:EARLY, 0:cols], dst_ref=o2rec,
                send_sem=edge_send.at[2], recv_sem=edge_recv.at[2],
                device_id=(row_at(-2), c), device_id_type=MESH,
            )
            near = pltpu.make_async_remote_copy(
                src_ref=osend, dst_ref=orec,
                send_sem=edge_send.at[1], recv_sem=edge_recv.at[1],
                device_id=(row_at(-1), c), device_id_type=MESH,
            )
            near.start()
            far.start()
            halo.wait_recv()
        frame = xe[WIDTH * f : WIDTH * f + FRAME, :]
        xe[WIDTH * f : WIDTH * f + FRAME, :] = frame - jnp.dot(
            products[f][0:FRAME, 0:FRAME], frame, precision=HIGH, preferred_element_type=jnp.float32
        )

    y_copy = pltpu.make_async_copy(xe.at[WIDTH : WIDTH + rows, :], y_ref, y_sem)
    y_copy.start()

    near.wait_recv()
    far.wait_recv()
    inflow_ref[0:8, :] = orec[0:8, 0:cols]
    inflow_ref[8:RIM, :] = orec[8:RIM, 0:cols] + jnp.dot(
        orec[8:RIM, cols : cols + EARLY], o2rec[...], precision=HIGH, preferred_element_type=jnp.float32
    )

    for copy in copies:
        copy.wait_send()
    halo.wait_send()
    near.wait_send()
    far.wait_send()
    y_copy.wait()


def finish_kernel(y_ref, inflow_ref, out_ref):
    cols = out_ref.shape[1]
    out_ref[...] = y_ref[:, 0:cols] + jnp.dot(
        y_ref[:, cols : cols + RIM], inflow_ref[...], precision=HIGH, preferred_element_type=jnp.float32
    )


def local(row_count, col_count, eig_slab, reflectors, row_offsets):
    rows, cols = eig_slab.shape
    per = reflectors.shape[0]
    wide = cols + LANES
    sends = 3 * col_count - 1
    y, inflow = pl.pallas_call(
        functools.partial(local_kernel, row_count, col_count),
        out_shape=(
            jax.ShapeDtypeStruct((rows, wide), jnp.float32),
            jax.ShapeDtypeStruct((RIM, cols), jnp.float32),
        ),
        in_specs=[
            pl.BlockSpec(memory_space=pltpu.SMEM),
            pl.BlockSpec(memory_space=pltpu.VMEM),
            pl.BlockSpec(memory_space=pl.ANY),
        ],
        out_specs=(pl.BlockSpec(memory_space=pl.ANY), pl.BlockSpec(memory_space=pltpu.VMEM)),
        scratch_shapes=[
            pltpu.VMEM((WIDTH + rows + RIM, wide), jnp.float32),
            pltpu.VMEM((col_count, per, rows + 2 * LANES), jnp.float32),
            pltpu.VMEM((SWEEPS, rows + 2 * LANES), jnp.float32),
            pltpu.VMEM((RIM, wide), jnp.float32),
            pltpu.VMEM((RIM, wide), jnp.float32),
            pltpu.VMEM((EARLY, cols), jnp.float32),
            pltpu.SemaphoreType.DMA,
            pltpu.SemaphoreType.DMA,
            pltpu.SemaphoreType.DMA((sends,)),
            pltpu.SemaphoreType.DMA((3 * col_count,)),
            pltpu.SemaphoreType.DMA((3,)),
            pltpu.SemaphoreType.DMA((3,)),
        ],
        compiler_params=pltpu.CompilerParams(
            collective_id=0, has_side_effects=True, vmem_limit_bytes=24 * 2**20
        ),
        name="sweep",
    )(row_offsets, reflectors, eig_slab)
    step = 128
    return pl.pallas_call(
        finish_kernel,
        out_shape=jax.ShapeDtypeStruct((rows, cols), jnp.float32),
        grid=(rows // step,),
        in_specs=[
            pl.BlockSpec((step, wide), lambda i: (i, 0)),
            pl.BlockSpec((RIM, cols), lambda i: (0, 0)),
        ],
        out_specs=pl.BlockSpec((step, cols), lambda i: (i, 0)),
        name="finish",
    )(y, inflow)


def solution(mesh):
    placed = (P("row", "col"), P("col", "row"), P())
    return jax.shard_map(
        functools.partial(local, mesh.shape["row"], mesh.shape["col"]),
        mesh=mesh, in_specs=placed, out_specs=P("row", "col"), check_vma=False,
    )
```

time: 268 us -> 37.4 us (0.14)
  the two profiles are of different devices: /device:TPU:6 before, /device:TPU:1 now
where the time goes in v1:
time: 37.4 us; the launch traced here: 37.1 us
  Pallas kernels  32.9 us (88%)
  local copies, waits for them, and re-layouts  4.24 us (11%)
    pallas_call x1, Pallas kernels, local(): pl.pallas_call(functools.partial(local_kernel, row_count, col_count), out...  29 us
    unnamed x10, local copies, waits for them, and re-layouts  4.24 us
    pallas_call x1, Pallas kernels, local(): pl.pallas_call(finish_kernel, out_shape=jax.ShapeDtypeStruct((rows, cols)...  3.87 us

profile of v1, /device:TPU:1, one launch (start us, length us, event | category | flops | bytes accessed | tf_op | source)
XLA Modules:
  0.0 37.1 jit_solution(6982926862002315027)
XLA Ops:
  0.0 0.0 copy-start.1
  0.0 1.2 %copy-done.1 = f32[512,512]{1,0:T(8,128)S(1)} copy-done((f32[512,512]{1,0:T(8,128)S(1)}, f32[512,512]{1,0:T(8,128)}, u32[]{:S(2)}) %copy-start.1) | copy-done | bytes 1048600
  1.2 0.0 copy-start.3
  1.2 0.7 %copy-done.3 = f32[2,512]{1,0:T(2,128)S(1)} copy-done((f32[2,512]{1,0:T(2,128)S(1)}, f32[2,512]{1,0:T(2,128)}, u32[]{:S(2)}) %copy-start.3) | copy-done | bytes 4120
  1.9 0.0 copy-start.4
  1.9 0.7 %copy-done.4 = s32[16]{0:T(128)S(1)} copy-done((s32[16]{0:T(128)S(1)}, s32[16]{0:T(128)}, u32[]{:S(2)}) %copy-start.4) | copy-done | bytes 88
  2.6 29.0 %sweep.1 = (f32[512,640]{1,0:T(8,128)S(1)}, f32[24,512]{1,0:T(8,128)S(1)}) custom-call(s32[16]{0:T(128)S(1)} %copy-done.4, f32[2,512]{1,0:T(2,128)S(1)} %copy-done.3, f32[512,512]{1,0:T(8,128)S(1)} %copy-done.1), custom_call_target="tpu_custom_call" | custom-call | tf_op jit(solution)/shard_map/sweep/pallas_call | solution.py:194
  31.6 0.0 copy-start
  31.6 1.1 %copy-done = f32[512,640]{1,0:T(8,128)} copy-done((f32[512,640]{1,0:T(8,128)}, f32[512,640]{1,0:T(8,128)S(1)}, u32[]{:S(2)}) %copy-start) | copy-done | bytes 1310744
  32.7 0.0 copy-start.2
  32.7 0.6 %copy-done.2 = f32[24,512]{1,0:T(8,128)} copy-done((f32[24,512]{1,0:T(8,128)}, f32[24,512]{1,0:T(8,128)S(1)}, u32[]{:S(2)}) %copy-start.2) | copy-done | bytes 49176
  33.3 3.9 %finish.1 = f32[512,512]{1,0:T(8,128)} custom-call(f32[512,640]{1,0:T(8,128)} %copy-done, f32[24,512]{1,0:T(8,128)} %copy-done.2), custom_call_target="tpu_custom_call" | custom-call | tf_op jit(solution)/shard_map/finish/pallas_call | solution.py:226
Async XLA Ops:
  0.0 1.2 %copy-start.1 = (f32[512,512]{1,0:T(8,128)S(1)}, f32[512,512]{1,0:T(8,128)}, u32[]{:S(2)}) copy-start(f32[512,512]{1,0:T(8,128)} %x_ref.1) | copy-start | bytes 3145732
  1.2 0.7 %copy-start.3 = (f32[2,512]{1,0:T(2,128)S(1)}, f32[2,512]{1,0:T(2,128)}, u32[]{:S(2)}) copy-start(f32[2,512]{1,0:T(2,128)} %refl_ref.1) | copy-start | bytes 12292
  1.9 0.7 %copy-start.4 = (s32[16]{0:T(128)S(1)}, s32[16]{0:T(128)}, u32[]{:S(2)}) copy-start(s32[16]{0:T(128)} %off_ref.1) | copy-start | bytes 196
  31.6 1.1 %copy-start = (f32[512,640]{1,0:T(8,128)}, f32[512,640]{1,0:T(8,128)S(1)}, u32[]{:S(2)}) copy-start(f32[512,640]{1,0:T(8,128)S(1)} %get-tuple-element.7.y_ref) | copy-start | bytes 3932164
  32.7 0.6 %copy-start.2 = (f32[24,512]{1,0:T(8,128)}, f32[24,512]{1,0:T(8,128)S(1)}, u32[]{:S(2)}) copy-start(f32[24,512]{1,0:T(8,128)S(1)} %get-tuple-element.8.inflow_ref) | copy-start | bytes 147460

commit v2 on v0

v2 whole, which is shorter than its diff:
```python
import functools

import jax
import jax.numpy as jnp
from jax import lax
from jax.experimental import pallas as pl
from jax.experimental.pallas import tpu as pltpu
from jax.sharding import PartitionSpec as P

WIDTH = 64
SWEEPS = 16
RIM = 24
FRAME = WIDTH + RIM
EARLY = 16
LANES = 128
TURN = 16
MESH = pl.DeviceIdType.MESH
F32 = jnp.float32
HIGH = lax.Precision.HIGH
HIGHEST = lax.Precision.HIGHEST


def dot(a, b, precision=HIGH):
    return jnp.dot(a, b, precision=precision, preferred_element_type=F32)


def halves(x):
    head = x.astype(jnp.bfloat16)
    return head, (x - head.astype(F32)).astype(jnp.bfloat16)


def substituted(scaled, base, w):
    half = SWEEPS // 2
    top, bottom = w[0:half], w[half:SWEEPS]
    for j in range(SWEEPS - 1):
        column = slice(base + j, base + j + 1)
        if j < half:
            row = top[j : j + 1]
            if j < half - 1:
                top = top - scaled[0:half, column] * row
        else:
            row = bottom[j - half : j - half + 1]
        bottom = bottom - scaled[half:SWEEPS, column] * row
    return jnp.concatenate([top, bottom], axis=0)


def combined(frames, taus):
    v_all = jnp.concatenate(frames, axis=0)
    tau = jnp.concatenate(taus, axis=0)
    n = v_all.shape[0]
    gram = lax.dot_general(
        v_all, v_all, (((1,), (1,)), ((), ())), precision=HIGHEST, preferred_element_type=F32
    )
    scaled = gram * tau
    w_all = v_all * tau
    out = []
    for i, v in enumerate(frames):
        lo = SWEEPS * i
        block = scaled[lo : lo + SWEEPS, 0:n]
        below = lax.broadcasted_iota(jnp.int32, (SWEEPS, n), 0) > (
            lax.broadcasted_iota(jnp.int32, (SWEEPS, n), 1) - lo
        )
        block = jnp.where(below, block, 0.0)
        w = substituted(block, lo, w_all[lo : lo + SWEEPS])
        vh, vl = halves(v)
        wh, wl = halves(w)
        product = lax.dot_general(
            jnp.concatenate([vh, vh, vl], axis=0), jnp.concatenate([wh, wl, wh], axis=0),
            (((0,), (0,)), ((), ())), preferred_element_type=F32,
        )
        out.append((w, product))
    return out


def sweep_kernel(
    row_count, col_count,
    off_hbm, refl_hbm, x_hbm,
    y_ref,
    off_ref, xe, vrec, vv, heads, tails, osend, orec, o2rec, first_product,
    local_sems, send_sems, recv_sems, edge_send, edge_recv, ready,
):
    per, rows = refl_hbm.shape
    cols = x_hbm.shape[1]
    wide = cols + LANES
    chains = rows // WIDTH
    b = lax.axis_index("row")
    c = lax.axis_index("col")
    below1, below2 = (b - 1, c), (b - 2, c)
    above1, above2 = (b + 1, c), (b + 2, c)
    has_below1, has_below2 = b >= 1, b >= 2
    has_above1, has_above2 = b < row_count - 1, b < row_count - 2
    far1 = lax.rem(b, TURN) == 0
    far2 = lax.rem(b, TURN) < 2

    def col_at(d):
        return lax.rem(c + d, col_count)

    barrier = pltpu.get_barrier_semaphore()

    def greet(peer):
        pl.semaphore_signal(barrier, inc=1, device_id=peer, device_id_type=MESH)

    order = sorted(range(1, col_count), key=lambda d: -min(d, col_count - d))
    for d in order:
        greet((b, col_at(d)))
    pl.when(has_below1)(lambda: greet(below1))
    pl.when(has_below2)(lambda: greet(below2))

    refl_copy = pltpu.make_async_copy(refl_hbm, vrec.at[c], local_sems.at[0])
    off_copy = pltpu.make_async_copy(off_hbm, off_ref, local_sems.at[1])
    x_copy = pltpu.make_async_copy(x_hbm, xe.at[WIDTH : WIDTH + rows, 0:cols], local_sems.at[2])
    refl_copy.start()
    off_copy.start()
    x_copy.start()

    xe[WIDTH + rows : WIDTH + rows + RIM, 0:cols] = jnp.zeros((RIM, cols), F32)
    xe[WIDTH : WIDTH + rows, cols:wide] = jnp.zeros((rows, LANES), F32)
    unit = lax.broadcasted_iota(jnp.int32, (RIM, LANES), 0) == lax.broadcasted_iota(
        jnp.int32, (RIM, LANES), 1
    )
    unit = jnp.where(unit, 1.0, 0.0)
    xe[WIDTH + rows : WIDTH + rows + RIM, cols:wide] = unit

    @pl.when(b == 0)
    def _():
        xe[0:WIDTH, 0:cols] = jnp.zeros((WIDTH, cols), F32)

    @pl.when(b == row_count - 1)
    def _():
        orec[...] = jnp.zeros((RIM, wide), F32)

    @pl.when(b >= row_count - 2)
    def _():
        o2rec[...] = jnp.zeros((EARLY, cols), F32)

    pl.semaphore_wait(
        barrier, col_count - 1 + has_above1.astype(jnp.int32) + has_above2.astype(jnp.int32)
    )

    gathers = []
    for d in order:
        copy = pltpu.make_async_remote_copy(
            src_ref=refl_hbm, dst_ref=vrec.at[c], send_sem=send_sems.at[d], recv_sem=recv_sems.at[d],
            device_id=(b, col_at(d)), device_id_type=MESH,
        )
        copy.start()
        gathers.append(copy)

    def edge(i, src, dst, peer):
        return pltpu.make_async_remote_copy(
            src_ref=src, dst_ref=dst, send_sem=edge_send.at[i], recv_sem=edge_recv.at[i],
            device_id=peer, device_id_type=MESH,
        )

    halo_copy = edge(0, x_hbm.at[rows - WIDTH : rows, :], xe.at[0:WIDTH, 0:cols], above1)
    tails_copy = edge(1, vv.at[:, rows - LANES : rows], tails, above1)
    heads_copy = edge(2, vv.at[:, 0:LANES], heads, below1)
    near_copy = edge(3, osend, orec, below1)
    far_copy = edge(4, osend.at[0:EARLY, 0:cols], o2rec, below2)

    def tell(i, peer):
        pl.semaphore_signal(ready.at[i], inc=1, device_id=peer, device_id_type=MESH)

    @pl.when(has_above1)
    def _():
        tell(0, above1)
        halo_copy.start()

    pl.when(has_above2)(lambda: tell(1, above2))

    refl_copy.wait()
    off_copy.wait()
    for copy in gathers:
        copy.wait_recv()
    for i in range(col_count):
        vv[i * per : (i + 1) * per, :] = vrec[i]

    def send_heads():
        pl.semaphore_wait(ready.at[0], 1)
        heads_copy.start()

    pl.when(has_above1)(tails_copy.start)
    pl.when(has_below1 & jnp.logical_not(far1))(send_heads)

    sweep_of = lax.broadcasted_iota(jnp.int32, (SWEEPS, LANES), 0)
    lane_of = lax.broadcasted_iota(jnp.int32, (SWEEPS, LANES), 1)
    first = jnp.zeros((SWEEPS, LANES), jnp.int32)
    for s in range(SWEEPS):
        first = jnp.where(sweep_of == s, off_ref[s], first)
    window = (lane_of >= first) & (lane_of < first + WIDTH)

    own = vv[...]
    turned = pltpu.roll(own, rows - WIDTH, 1)
    frames = []
    for k in range(chains - 1):
        lo = WIDTH * k
        v = own[:, lo : lo + LANES] if k % 2 == 0 else turned[:, lo - WIDTH : lo - WIDTH + LANES]
        frames.append(jnp.where(window, v, 0.0))
    taus = [2.0 / jnp.sum(v * v, axis=1, keepdims=True) for v in frames]
    products = [product for _, product in combined(frames, taus)]

    x_copy.wait()
    form = unit - products[0][0:RIM]
    outflow = dot(form[:, 0:WIDTH], xe[WIDTH : 2 * WIDTH, 0:cols])
    for k in range(1, chains - 1):
        form = dot(form[:, WIDTH:FRAME], unit - products[k][0:RIM])
        outflow = outflow + dot(form[:, 0:WIDTH], xe[WIDTH * (k + 1) : WIDTH * (k + 2), 0:cols])
    onward = form[:, WIDTH:FRAME]

    pl.when(has_above1)(heads_copy.wait_recv)
    v = jnp.concatenate([own[:, rows - WIDTH : rows], heads[:, 0:WIDTH]], axis=1)
    v = jnp.where(window & ((lane_of < WIDTH) | has_above1), v, 0.0)
    tau = 2.0 / jnp.sum(v * v, axis=1, keepdims=True)
    ((_, product),) = combined([v], [tau])
    products.append(product)
    form = dot(onward, unit - product[0:RIM])
    osend[:, 0:cols] = outflow + dot(form[:, 0:WIDTH], xe[rows : rows + WIDTH, 0:cols])
    osend[:, cols:wide] = jnp.concatenate([form[:, WIDTH:LANES], jnp.zeros((RIM, WIDTH), F32)], axis=1)

    def send_far():
        pl.semaphore_wait(ready.at[1], 1)
        far_copy.start()

    pl.when(has_below1 & jnp.logical_not(far1))(near_copy.start)
    pl.when(has_below2 & jnp.logical_not(far2))(send_far)

    def lower_chain():
        pl.when(has_below1)(tails_copy.wait_recv)
        v = jnp.concatenate([tails[:, WIDTH:LANES], vv[:, 0:WIDTH]], axis=1)
        v = jnp.where(window & has_below1, v, 0.0)
        dead = jnp.where(has_below1, 0.0, 1.0)
        tau = jnp.where(has_below1, 2.0 / (jnp.sum(v * v, axis=1, keepdims=True) + dead), 0.0)
        ((_, product),) = combined([v], [tau])
        first_product[...] = product[WIDTH:FRAME]

    pl.when(jnp.logical_not(far1))(lower_chain)

    for k in range(chains - 1, -1, -1):
        lo = WIDTH * (k + 1)
        frame = xe[lo : lo + FRAME, :]
        xe[lo : lo + FRAME, :] = frame - dot(products[k][0:FRAME, 0:FRAME], frame)

    @pl.when(has_below1 & far1)
    def _():
        send_heads()
        near_copy.start()

    pl.when(has_below2 & far2)(send_far)

    pl.when(has_above1)(near_copy.wait_recv)
    pl.when(has_above2)(far_copy.wait_recv)
    early = RIM - EARLY
    inflow = jnp.concatenate(
        [
            orec[0:early, 0:cols],
            orec[early:RIM, 0:cols] + dot(orec[early:RIM, cols : cols + EARLY], o2rec[...]),
        ],
        axis=0,
    )
    y_ref[...] = xe[WIDTH : WIDTH + rows, 0:cols] + dot(
        xe[WIDTH : WIDTH + rows, cols : cols + RIM], inflow
    )

    pl.when(far1)(lower_chain)
    pl.when(has_below1)(halo_copy.wait_recv)
    frame = jnp.concatenate([xe[0:WIDTH, 0:cols], y_ref[0:RIM, :]], axis=0)
    y_ref[0:RIM, :] = y_ref[0:RIM, :] - dot(first_product[:, 0:FRAME], frame)

    for copy in gathers:
        copy.wait_send()

    @pl.when(has_above1)
    def _():
        halo_copy.wait_send()
        tails_copy.wait_send()

    @pl.when(has_below1)
    def _():
        heads_copy.wait_send()
        near_copy.wait_send()

    pl.when(has_below2)(far_copy.wait_send)


def local(row_count, col_count, eig_slab, reflectors, row_offsets):
    rows, cols = eig_slab.shape
    per = reflectors.shape[0]
    wide = cols + LANES
    return pl.pallas_call(
        functools.partial(sweep_kernel, row_count, col_count),
        out_shape=jax.ShapeDtypeStruct((rows, cols), F32),
        in_specs=[pl.BlockSpec(memory_space=pltpu.HBM)] * 3,
        out_specs=pl.BlockSpec(memory_space=pltpu.VMEM),
        scratch_shapes=[
            pltpu.SMEM((SWEEPS,), jnp.int32),
            pltpu.VMEM((WIDTH + rows + RIM, wide), F32),
            pltpu.VMEM((col_count, per, rows), F32),
            pltpu.VMEM((SWEEPS, rows), F32),
            pltpu.VMEM((SWEEPS, LANES), F32),
            pltpu.VMEM((SWEEPS, LANES), F32),
            pltpu.VMEM((RIM, wide), F32),
            pltpu.VMEM((RIM, wide), F32),
            pltpu.VMEM((EARLY, cols), F32),
            pltpu.VMEM((RIM, LANES), F32),
            pltpu.SemaphoreType.DMA((3,)),
            pltpu.SemaphoreType.DMA((col_count,)),
            pltpu.SemaphoreType.DMA((col_count,)),
            pltpu.SemaphoreType.DMA((5,)),
            pltpu.SemaphoreType.DMA((5,)),
            pltpu.SemaphoreType.REGULAR((2,)),
        ],
        compiler_params=pltpu.CompilerParams(
            collective_id=0, has_side_effects=True, vmem_limit_bytes=24 * 2**20
        ),
        name="sweep",
    )(*(pltpu.with_memory_space_constraint(a, pltpu.HBM) for a in (row_offsets, reflectors, eig_slab)))


def solution(mesh):
    placed = (P("row", "col"), P("col", "row"), P())
    return jax.shard_map(
        functools.partial(local, mesh.shape["row"], mesh.shape["col"]),
        mesh=mesh, in_specs=placed, out_specs=P("row", "col"), check_vma=False,
    )
```

time: 268 us -> 22.5 us (0.08)
  the two profiles are of different devices: /device:TPU:6 before, /device:TPU:132 now
where the time goes in v2:
time: 22.5 us; the launch traced here: 22.3 us
  Pallas kernels  21.4 us (95%)
  local copies, waits for them, and re-layouts  0.97 us (4%)
    pallas_call x1, Pallas kernels, local(): pl.pallas_call(functools.partial(sweep_kernel, row_count, col_count), out...  21.4 us
    unnamed x1, local copies, waits for them, and re-layouts  0.97 us

profile of v2, /device:TPU:132, one launch (start us, length us, event | category | flops | bytes accessed | tf_op | source)
XLA Modules:
  0.0 22.3 jit_solution(10410737382488373512)
XLA Ops:
  0.0 21.4 %sweep.1 = f32[512,512]{1,0:T(8,128)S(1)} custom-call(s32[16]{0:T(128)} %off_hbm.1, f32[2,512]{1,0:T(2,128)} %refl_hbm.1, f32[512,512]{1,0:T(8,128)} %x_hbm.1), custom_call_target="tpu_custom_call" | custom-call | tf_op jit(solution)/shard_map/sweep/pallas_call | solution.py:289
  21.4 1.0 %copy.5 = f32[512,512]{1,0:T(8,128)} copy(f32[512,512]{1,0:T(8,128)S(1)} %sweep.1) | data formatting | bytes 2097152

commit v3 on v2

--- a/solution.py
+++ b/solution.py
@@ -76,7 +76,7 @@
     row_count, col_count,
     off_hbm, refl_hbm, x_hbm,
     y_ref,
-    off_ref, xe, vrec, vv, heads, tails, osend, orec, o2rec, first_product,
+    off_ref, xe, vrec, vv, heads, tails, osend, fsend, orec, o2rec, first_product,
     local_sems, send_sems, recv_sems, edge_send, edge_recv, ready,
 ):
     per, rows = refl_hbm.shape
@@ -89,8 +89,17 @@
     above1, above2 = (b + 1, c), (b + 2, c)
     has_below1, has_below2 = b >= 1, b >= 2
     has_above1, has_above2 = b < row_count - 1, b < row_count - 2
-    far1 = lax.rem(b, TURN) == 0
-    far2 = lax.rem(b, TURN) < 2
+    place = lax.rem(b, TURN)
+    late_below1, late_below2 = has_below1 & (place == 0), has_below2 & (place < 2)
+    late_above1, late_above2 = has_above1 & (place < TURN - 1), has_above2 & (place < TURN - 2)
+    soon_below1, soon_below2 = has_below1 & (place > 0), has_below2 & (place > 1)
+    soon_above1, soon_above2 = has_above1 & (place == TURN - 1), has_above2 & (place >= TURN - 2)
+    neighbours = (
+        (above1, late_above1, soon_above1, 0),
+        (above2, late_above2, soon_above2, 1),
+        (below1, late_below1, soon_below1, 2),
+        (below2, late_below2, soon_below2, 3),
+    )
 
     def col_at(d):
         return lax.rem(c + d, col_count)
@@ -103,8 +112,8 @@
     order = sorted(range(1, col_count), key=lambda d: -min(d, col_count - d))
     for d in order:
         greet((b, col_at(d)))
-    pl.when(has_below1)(lambda: greet(below1))
-    pl.when(has_below2)(lambda: greet(below2))
+    for peer, late, _, _ in neighbours:
+        pl.when(late)(functools.partial(greet, peer))
 
     refl_copy = pltpu.make_async_copy(refl_hbm, vrec.at[c], local_sems.at[0])
     off_copy = pltpu.make_async_copy(off_hbm, off_ref, local_sems.at[1])
@@ -133,9 +142,10 @@
     def _():
         o2rec[...] = jnp.zeros((EARLY, cols), F32)
 
-    pl.semaphore_wait(
-        barrier, col_count - 1 + has_above1.astype(jnp.int32) + has_above2.astype(jnp.int32)
-    )
+    greeted = col_count - 1
+    for _, _, soon, _ in neighbours:
+        greeted = greeted + soon.astype(jnp.int32)
+    pl.semaphore_wait(barrier, greeted)
 
     gathers = []
     for d in order:
@@ -156,17 +166,16 @@
     tails_copy = edge(1, vv.at[:, rows - LANES : rows], tails, above1)
     heads_copy = edge(2, vv.at[:, 0:LANES], heads, below1)
     near_copy = edge(3, osend, orec, below1)
-    far_copy = edge(4, osend.at[0:EARLY, 0:cols], o2rec, below2)
+    far_copy = edge(4, fsend, o2rec, below2)
 
     def tell(i, peer):
         pl.semaphore_signal(ready.at[i], inc=1, device_id=peer, device_id_type=MESH)
 
-    @pl.when(has_above1)
-    def _():
-        tell(0, above1)
-        halo_copy.start()
-
-    pl.when(has_above2)(lambda: tell(1, above2))
+    for peer, _, soon, i in neighbours:
+        pl.when(soon)(functools.partial(tell, (i + 2) % 4, peer))
+
+    def heard(i):
+        pl.semaphore_wait(ready.at[i], 1)
 
     refl_copy.wait()
     off_copy.wait()
@@ -175,12 +184,12 @@
     for i in range(col_count):
         vv[i * per : (i + 1) * per, :] = vrec[i]
 
-    def send_heads():
-        pl.semaphore_wait(ready.at[0], 1)
-        heads_copy.start()
-
-    pl.when(has_above1)(tails_copy.start)
-    pl.when(has_below1 & jnp.logical_not(far1))(send_heads)
+    pl.when(soon_below1)(heads_copy.start)
+
+    @pl.when(soon_above1)
+    def _():
+        tails_copy.start()
+        halo_copy.start()
 
     sweep_of = lax.broadcasted_iota(jnp.int32, (SWEEPS, LANES), 0)
     lane_of = lax.broadcasted_iota(jnp.int32, (SWEEPS, LANES), 1)
@@ -207,6 +216,17 @@
         outflow = outflow + dot(form[:, 0:WIDTH], xe[WIDTH * (k + 1) : WIDTH * (k + 2), 0:cols])
     onward = form[:, WIDTH:FRAME]
 
+    fsend[...] = outflow[0:EARLY] + dot(onward[0:EARLY], xe[rows : rows + RIM, 0:cols])
+    pl.when(soon_below2)(far_copy.start)
+
+    @pl.when(late_above1)
+    def _():
+        heard(0)
+        tails_copy.start()
+        halo_copy.start()
+
+    pl.when(late_above2)(lambda: heard(1))
+
     pl.when(has_above1)(heads_copy.wait_recv)
     v = jnp.concatenate([own[:, rows - WIDTH : rows], heads[:, 0:WIDTH]], axis=1)
     v = jnp.where(window & ((lane_of < WIDTH) | has_above1), v, 0.0)
@@ -217,12 +237,7 @@
     osend[:, 0:cols] = outflow + dot(form[:, 0:WIDTH], xe[rows : rows + WIDTH, 0:cols])
     osend[:, cols:wide] = jnp.concatenate([form[:, WIDTH:LANES], jnp.zeros((RIM, WIDTH), F32)], axis=1)
 
-    def send_far():
-        pl.semaphore_wait(ready.at[1], 1)
-        far_copy.start()
-
-    pl.when(has_below1 & jnp.logical_not(far1))(near_copy.start)
-    pl.when(has_below2 & jnp.logical_not(far2))(send_far)
+    pl.when(soon_below1)(near_copy.start)
 
     def lower_chain():
         pl.when(has_below1)(tails_copy.wait_recv)
@@ -233,19 +248,23 @@
         ((_, product),) = combined([v], [tau])
         first_product[...] = product[WIDTH:FRAME]
 
-    pl.when(jnp.logical_not(far1))(lower_chain)
+    pl.when(place > 0)(lower_chain)
 
     for k in range(chains - 1, -1, -1):
         lo = WIDTH * (k + 1)
         frame = xe[lo : lo + FRAME, :]
         xe[lo : lo + FRAME, :] = frame - dot(products[k][0:FRAME, 0:FRAME], frame)
 
-    @pl.when(has_below1 & far1)
-    def _():
-        send_heads()
+    @pl.when(late_below1)
+    def _():
+        heard(2)
+        heads_copy.start()
         near_copy.start()
 
-    pl.when(has_below2 & far2)(send_far)
+    @pl.when(late_below2)
+    def _():
+        heard(3)
+        far_copy.start()
 
     pl.when(has_above1)(near_copy.wait_recv)
     pl.when(has_above2)(far_copy.wait_recv)
@@ -261,7 +280,7 @@
         xe[WIDTH : WIDTH + rows, cols : cols + RIM], inflow
     )
 
-    pl.when(far1)(lower_chain)
+    pl.when(place == 0)(lower_chain)
     pl.when(has_below1)(halo_copy.wait_recv)
     frame = jnp.concatenate([xe[0:WIDTH, 0:cols], y_ref[0:RIM, :]], axis=0)
     y_ref[0:RIM, :] = y_ref[0:RIM, :] - dot(first_product[:, 0:FRAME], frame)
@@ -299,6 +318,7 @@
             pltpu.VMEM((SWEEPS, LANES), F32),
             pltpu.VMEM((SWEEPS, LANES), F32),
             pltpu.VMEM((RIM, wide), F32),
+            pltpu.VMEM((EARLY, cols), F32),
             pltpu.VMEM((RIM, wide), F32),
             pltpu.VMEM((EARLY, cols), F32),
             pltpu.VMEM((RIM, LANES), F32),
@@ -307,7 +327,7 @@
             pltpu.SemaphoreType.DMA((col_count,)),
             pltpu.SemaphoreType.DMA((5,)),
             pltpu.SemaphoreType.DMA((5,)),
-            pltpu.SemaphoreType.REGULAR((2,)),
+            pltpu.SemaphoreType.REGULAR((4,)),
         ],
         compiler_params=pltpu.CompilerParams(
             collective_id=0, has_side_effects=True, vmem_limit_bytes=24 * 2**20

time: 22.5 us -> 22.7 us (level)
  the two profiles are of different devices: /device:TPU:132 before, /device:TPU:1 now
where the time goes in v3:
time: 22.7 us; the launch traced here: 22.5 us
  Pallas kernels  21.5 us (95%)
  local copies, waits for them, and re-layouts  0.97 us (4%)
    pallas_call x1, Pallas kernels, local(): pl.pallas_call(functools.partial(sweep_kernel, row_count, col_count), out...  21.5 us
    unnamed x1, local copies, waits for them, and re-layouts  0.97 us

profile of v3, /device:TPU:1, one launch (start us, length us, event | category | flops | bytes accessed | tf_op | source)
XLA Modules:
  0.0 22.5 jit_solution(13163384183175625723)
XLA Ops:
  0.0 21.5 %sweep.1 = f32[512,512]{1,0:T(8,128)S(1)} custom-call(s32[16]{0:T(128)} %off_hbm.1, f32[2,512]{1,0:T(2,128)} %refl_hbm.1, f32[512,512]{1,0:T(8,128)} %x_hbm.1), custom_call_target="tpu_custom_call" | custom-call | tf_op jit(solution)/shard_map/sweep/pallas_call | solution.py:308
  21.5 1.0 %copy.5 = f32[512,512]{1,0:T(8,128)} copy(f32[512,512]{1,0:T(8,128)S(1)} %sweep.1) | data formatting | bytes 2097152

commit v4 on v3

--- a/solution.py
+++ b/solution.py
@@ -76,8 +76,8 @@
     row_count, col_count,
     off_hbm, refl_hbm, x_hbm,
     y_ref,
-    off_ref, xe, vrec, vv, heads, tails, osend, fsend, orec, o2rec, first_product,
-    local_sems, send_sems, recv_sems, edge_send, edge_recv, ready,
+    off_ref, xe, vrec, vv, heads, tails, tv, osend, fsend, orec, o2rec, first_product,
+    local_sems, send_sems, recv_sems, tail_send, tail_recv, edge_send, edge_recv, ready,
 ):
     per, rows = refl_hbm.shape
     cols = x_hbm.shape[1]
@@ -90,10 +90,16 @@
     has_below1, has_below2 = b >= 1, b >= 2
     has_above1, has_above2 = b < row_count - 1, b < row_count - 2
     place = lax.rem(b, TURN)
-    late_below1, late_below2 = has_below1 & (place == 0), has_below2 & (place < 2)
-    late_above1, late_above2 = has_above1 & (place < TURN - 1), has_above2 & (place < TURN - 2)
-    soon_below1, soon_below2 = has_below1 & (place > 0), has_below2 & (place > 1)
-    soon_above1, soon_above2 = has_above1 & (place == TURN - 1), has_above2 & (place >= TURN - 2)
+    late_below1 = has_below1 & ((place == 0) | (b == 1))
+    late_below2 = has_below2 & ((place < 2) | (b == 2))
+    late_above1 = has_above1 & (place < TURN - 1) & (b > 0)
+    late_above2 = has_above2 & (place < TURN - 2) & (b > 0)
+    soon_below1, soon_below2 = has_below1 & jnp.logical_not(late_below1), has_below2 & jnp.logical_not(late_below2)
+    soon_above1, soon_above2 = has_above1 & jnp.logical_not(late_above1), has_above2 & jnp.logical_not(late_above2)
+    last_below1, last_below2 = late_below1 & (place == 0), late_below2 & (place < 2)
+    next_below1, next_below2 = late_below1 & (place > 0), late_below2 & (place > 1)
+    lower_last = (place == 0) | (b == 1)
+    wide_above1 = soon_above1 & (place == TURN - 1)
     neighbours = (
         (above1, late_above1, soon_above1, 0),
         (above2, late_above2, soon_above2, 1),
@@ -101,19 +107,26 @@
         (below2, late_below2, soon_below2, 3),
     )
 
+    barrier = pltpu.get_barrier_semaphore()
+
+    def greet(peer):
+        pl.semaphore_signal(barrier, inc=1, device_id=peer, device_id_type=MESH)
+
     def col_at(d):
         return lax.rem(c + d, col_count)
-
-    barrier = pltpu.get_barrier_semaphore()
-
-    def greet(peer):
-        pl.semaphore_signal(barrier, inc=1, device_id=peer, device_id_type=MESH)
 
     order = sorted(range(1, col_count), key=lambda d: -min(d, col_count - d))
     for d in order:
         greet((b, col_at(d)))
-    for peer, late, _, _ in neighbours:
+    for i, (peer, late, _, _) in enumerate(neighbours):
+        if i == 2:
+            late = next_below1
         pl.when(late)(functools.partial(greet, peer))
+
+    @pl.when(last_below1)
+    def _():
+        for d in range(col_count):
+            greet((b - 1, col_at(d)))
 
     refl_copy = pltpu.make_async_copy(refl_hbm, vrec.at[c], local_sems.at[0])
     off_copy = pltpu.make_async_copy(off_hbm, off_ref, local_sems.at[1])
@@ -142,19 +155,21 @@
     def _():
         o2rec[...] = jnp.zeros((EARLY, cols), F32)
 
-    greeted = col_count - 1
+    greeted = jnp.where(wide_above1, 2 * (col_count - 1), col_count - 1)
     for _, _, soon, _ in neighbours:
         greeted = greeted + soon.astype(jnp.int32)
     pl.semaphore_wait(barrier, greeted)
 
-    gathers = []
-    for d in order:
-        copy = pltpu.make_async_remote_copy(
-            src_ref=refl_hbm, dst_ref=vrec.at[c], send_sem=send_sems.at[d], recv_sem=recv_sems.at[d],
+    refl_copy.wait()
+    gathers = [
+        pltpu.make_async_remote_copy(
+            src_ref=vrec.at[c], dst_ref=vrec.at[c], send_sem=send_sems.at[d], recv_sem=recv_sems.at[d],
             device_id=(b, col_at(d)), device_id_type=MESH,
         )
+        for d in order
+    ]
+    for copy in gathers:
         copy.start()
-        gathers.append(copy)
 
     def edge(i, src, dst, peer):
         return pltpu.make_async_remote_copy(
@@ -163,7 +178,15 @@
         )
 
     halo_copy = edge(0, x_hbm.at[rows - WIDTH : rows, :], xe.at[0:WIDTH, 0:cols], above1)
-    tails_copy = edge(1, vv.at[:, rows - LANES : rows], tails, above1)
+    tails_copy = edge(1, vrec.at[:, :, rows - LANES : rows], tails, above1)
+    tail_copies = [
+        pltpu.make_async_remote_copy(
+            src_ref=vrec.at[c, :, rows - LANES : rows], dst_ref=tails.at[c],
+            send_sem=tail_send.at[d], recv_sem=tail_recv.at[d],
+            device_id=(b + 1, col_at(d)), device_id_type=MESH,
+        )
+        for d in range(col_count)
+    ]
     heads_copy = edge(2, vv.at[:, 0:LANES], heads, below1)
     near_copy = edge(3, osend, orec, below1)
     far_copy = edge(4, fsend, o2rec, below2)
@@ -177,7 +200,14 @@
     def heard(i):
         pl.semaphore_wait(ready.at[i], 1)
 
-    refl_copy.wait()
+    @pl.when(wide_above1)
+    def _():
+        for copy in tail_copies:
+            copy.start()
+
+    pl.when(soon_above1)(halo_copy.start)
+
+
     off_copy.wait()
     for copy in gathers:
         copy.wait_recv()
@@ -186,10 +216,7 @@
 
     pl.when(soon_below1)(heads_copy.start)
 
-    @pl.when(soon_above1)
-    def _():
-        tails_copy.start()
-        halo_copy.start()
+    pl.when(soon_above1 & jnp.logical_not(wide_above1))(tails_copy.start)
 
     sweep_of = lax.broadcasted_iota(jnp.int32, (SWEEPS, LANES), 0)
     lane_of = lax.broadcasted_iota(jnp.int32, (SWEEPS, LANES), 1)
@@ -208,6 +235,19 @@
     taus = [2.0 / jnp.sum(v * v, axis=1, keepdims=True) for v in frames]
     products = [product for _, product in combined(frames, taus)]
 
+    @pl.when(late_above1)
+    def _():
+        heard(0)
+        tails_copy.start()
+        halo_copy.start()
+
+    pl.when(late_above2)(lambda: heard(1))
+
+    @pl.when(next_below1)
+    def _():
+        heard(2)
+        heads_copy.start()
+
     x_copy.wait()
     form = unit - products[0][0:RIM]
     outflow = dot(form[:, 0:WIDTH], xe[WIDTH : 2 * WIDTH, 0:cols])
@@ -217,15 +257,8 @@
     onward = form[:, WIDTH:FRAME]
 
     fsend[...] = outflow[0:EARLY] + dot(onward[0:EARLY], xe[rows : rows + RIM, 0:cols])
-    pl.when(soon_below2)(far_copy.start)
-
-    @pl.when(late_above1)
-    def _():
-        heard(0)
-        tails_copy.start()
-        halo_copy.start()
-
-    pl.when(late_above2)(lambda: heard(1))
+    pl.when(next_below2)(lambda: heard(3))
+    pl.when(soon_below2 | next_below2)(far_copy.start)
 
     pl.when(has_above1)(heads_copy.wait_recv)
     v = jnp.concatenate([own[:, rows - WIDTH : rows], heads[:, 0:WIDTH]], axis=1)
@@ -237,31 +270,40 @@
     osend[:, 0:cols] = outflow + dot(form[:, 0:WIDTH], xe[rows : rows + WIDTH, 0:cols])
     osend[:, cols:wide] = jnp.concatenate([form[:, WIDTH:LANES], jnp.zeros((RIM, WIDTH), F32)], axis=1)
 
-    pl.when(soon_below1)(near_copy.start)
+    pl.when(soon_below1 | next_below1)(near_copy.start)
 
     def lower_chain():
-        pl.when(has_below1)(tails_copy.wait_recv)
-        v = jnp.concatenate([tails[:, WIDTH:LANES], vv[:, 0:WIDTH]], axis=1)
+        pl.when(has_below1 & jnp.logical_not(last_below1))(tails_copy.wait_recv)
+
+        @pl.when(last_below1)
+        def _():
+            for copy in tail_copies:
+                copy.wait_recv()
+
+        for i in range(col_count):
+            tv[i * per : (i + 1) * per, :] = tails[i]
+        v = jnp.concatenate([tv[:, WIDTH:LANES], vv[:, 0:WIDTH]], axis=1)
         v = jnp.where(window & has_below1, v, 0.0)
         dead = jnp.where(has_below1, 0.0, 1.0)
         tau = jnp.where(has_below1, 2.0 / (jnp.sum(v * v, axis=1, keepdims=True) + dead), 0.0)
         ((_, product),) = combined([v], [tau])
         first_product[...] = product[WIDTH:FRAME]
 
-    pl.when(place > 0)(lower_chain)
 
     for k in range(chains - 1, -1, -1):
         lo = WIDTH * (k + 1)
         frame = xe[lo : lo + FRAME, :]
         xe[lo : lo + FRAME, :] = frame - dot(products[k][0:FRAME, 0:FRAME], frame)
 
-    @pl.when(late_below1)
+    pl.when(jnp.logical_not(lower_last))(lower_chain)
+
+    @pl.when(last_below1)
     def _():
         heard(2)
         heads_copy.start()
         near_copy.start()
 
-    @pl.when(late_below2)
+    @pl.when(last_below2)
     def _():
         heard(3)
         far_copy.start()
@@ -280,7 +322,7 @@
         xe[WIDTH : WIDTH + rows, cols : cols + RIM], inflow
     )
 
-    pl.when(place == 0)(lower_chain)
+    pl.when(lower_last)(lower_chain)
     pl.when(has_below1)(halo_copy.wait_recv)
     frame = jnp.concatenate([xe[0:WIDTH, 0:cols], y_ref[0:RIM, :]], axis=0)
     y_ref[0:RIM, :] = y_ref[0:RIM, :] - dot(first_product[:, 0:FRAME], frame)
@@ -288,10 +330,13 @@
     for copy in gathers:
         copy.wait_send()
 
-    @pl.when(has_above1)
-    def _():
-        halo_copy.wait_send()
-        tails_copy.wait_send()
+    pl.when(has_above1)(halo_copy.wait_send)
+    pl.when(has_above1 & jnp.logical_not(wide_above1))(tails_copy.wait_send)
+
+    @pl.when(wide_above1)
+    def _():
+        for copy in tail_copies:
+            copy.wait_send()
 
     @pl.when(has_below1)
     def _():
@@ -316,6 +361,7 @@
             pltpu.VMEM((col_count, per, rows), F32),
             pltpu.VMEM((SWEEPS, rows), F32),
             pltpu.VMEM((SWEEPS, LANES), F32),
+            pltpu.VMEM((col_count, per, LANES), F32),
             pltpu.VMEM((SWEEPS, LANES), F32),
             pltpu.VMEM((RIM, wide), F32),
             pltpu.VMEM((EARLY, cols), F32),
@@ -323,6 +369,8 @@
             pltpu.VMEM((EARLY, cols), F32),
             pltpu.VMEM((RIM, LANES), F32),
             pltpu.SemaphoreType.DMA((3,)),
+            pltpu.SemaphoreType.DMA((col_count,)),
+            pltpu.SemaphoreType.DMA((col_count,)),
             pltpu.SemaphoreType.DMA((col_count,)),
             pltpu.SemaphoreType.DMA((col_count,)),
             pltpu.SemaphoreType.DMA((5,)),

time: 22.7 us -> 20.5 us (0.903)
  Pallas kernels: 21.5 us -> 19.4 us
    pallas_call x1, Pallas kernels: 21.5 us -> 19.4 us  [local(): pl.pallas_call(functools.partial(sweep_kernel, row_count, col_count), out...]
where the time goes in v4:
time: 20.5 us; the launch traced here: 20.3 us
  Pallas kernels  19.4 us (95%)
  local copies, waits for them, and re-layouts  0.97 us (5%)
    pallas_call x1, Pallas kernels, local(): pl.pallas_call(functools.partial(sweep_kernel, row_count, col_count), out...  19.4 us
    unnamed x1, local copies, waits for them, and re-layouts  0.97 us

profile of v4, /device:TPU:1, one launch (start us, length us, event | category | flops | bytes accessed | tf_op | source)
XLA Modules:
  0.0 20.3 jit_solution(4645099473338791962)
XLA Ops:
  0.0 19.4 %sweep.1 = f32[512,512]{1,0:T(8,128)S(1)} custom-call(s32[16]{0:T(128)} %off_hbm.1, f32[2,512]{1,0:T(2,128)} %refl_hbm.1, f32[512,512]{1,0:T(8,128)} %x_hbm.1), custom_call_target="tpu_custom_call" | custom-call | tf_op jit(solution)/shard_map/sweep/pallas_call | solution.py:353
  19.4 1.0 %copy.5 = f32[512,512]{1,0:T(8,128)} copy(f32[512,512]{1,0:T(8,128)S(1)} %sweep.1) | data formatting | bytes 2097152

commit v5 on v4

--- a/solution.py
+++ b/solution.py
@@ -13,6 +13,7 @@
 FRAME = WIDTH + RIM
 EARLY = 16
 LANES = 128
+SLOT = 32
 TURN = 16
 MESH = pl.DeviceIdType.MESH
 F32 = jnp.float32
@@ -72,11 +73,23 @@
     return out
 
 
+def paired(upper, lower):
+    lanes = upper.shape[1]
+    entry = lax.broadcasted_iota(jnp.int32, (RIM, lanes), 0) == lax.broadcasted_iota(
+        jnp.int32, (RIM, lanes), 1
+    )
+    passed = jnp.where(entry, 1.0, 0.0) - upper[0:RIM]
+    right = dot(lower[0:FRAME, WIDTH:FRAME], passed)
+    right = jnp.concatenate([right[0:WIDTH], right[WIDTH:FRAME] + upper[0:RIM], upper[RIM:FRAME]], axis=0)
+    left = jnp.concatenate([lower[0:FRAME, 0:WIDTH], jnp.zeros((WIDTH, WIDTH), F32)], axis=0)
+    return jnp.concatenate([left, right[:, 0:FRAME]], axis=1)
+
+
 def sweep_kernel(
     row_count, col_count,
     off_hbm, refl_hbm, x_hbm,
     y_ref,
-    off_ref, xe, vrec, vv, heads, tails, tv, osend, fsend, orec, o2rec, first_product,
+    off_ref, xe, vrec, vv, heads, tails, tv, osend, fsend, orec, o2rec, first_product, upper, single, pairs, reply,
     local_sems, send_sems, recv_sems, tail_send, tail_recv, edge_send, edge_recv, ready,
 ):
     per, rows = refl_hbm.shape
@@ -135,13 +148,11 @@
     off_copy.start()
     x_copy.start()
 
-    xe[WIDTH + rows : WIDTH + rows + RIM, 0:cols] = jnp.zeros((RIM, cols), F32)
-    xe[WIDTH : WIDTH + rows, cols:wide] = jnp.zeros((rows, LANES), F32)
+    xe[:, cols:wide] = jnp.zeros((WIDTH + rows, LANES), F32)
     unit = lax.broadcasted_iota(jnp.int32, (RIM, LANES), 0) == lax.broadcasted_iota(
         jnp.int32, (RIM, LANES), 1
     )
-    unit = jnp.where(unit, 1.0, 0.0)
-    xe[WIDTH + rows : WIDTH + rows + RIM, cols:wide] = unit
+    rim = jnp.concatenate([jnp.zeros((RIM, cols), F32), jnp.where(unit, 1.0, 0.0)], axis=1)
 
     @pl.when(b == 0)
     def _():
@@ -195,7 +206,8 @@
         pl.semaphore_signal(ready.at[i], inc=1, device_id=peer, device_id_type=MESH)
 
     for peer, _, soon, i in neighbours:
-        pl.when(soon)(functools.partial(tell, (i + 2) % 4, peer))
+        if i != 3:
+            pl.when(soon)(functools.partial(tell, (i + 2) % 4, peer))
 
     def heard(i):
         pl.semaphore_wait(ready.at[i], 1)
@@ -217,6 +229,14 @@
     pl.when(soon_below1)(heads_copy.start)
 
     pl.when(soon_above1 & jnp.logical_not(wide_above1))(tails_copy.start)
+
+    def send_up():
+        heard(0)
+        tails_copy.start()
+        halo_copy.start()
+
+    slow_above1 = late_above1 & (place == TURN // 2 - 1)
+    pl.when(late_above1 & jnp.logical_not(slow_above1))(send_up)
 
     sweep_of = lax.broadcasted_iota(jnp.int32, (SWEEPS, LANES), 0)
     lane_of = lax.broadcasted_iota(jnp.int32, (SWEEPS, LANES), 1)
@@ -225,52 +245,93 @@
         first = jnp.where(sweep_of == s, off_ref[s], first)
     window = (lane_of >= first) & (lane_of < first + WIDTH)
 
-    own = vv[...]
-    turned = pltpu.roll(own, rows - WIDTH, 1)
-    frames = []
-    for k in range(chains - 1):
-        lo = WIDTH * k
-        v = own[:, lo : lo + LANES] if k % 2 == 0 else turned[:, lo - WIDTH : lo - WIDTH + LANES]
-        frames.append(jnp.where(window, v, 0.0))
-    taus = [2.0 / jnp.sum(v * v, axis=1, keepdims=True) for v in frames]
-    products = [product for _, product in combined(frames, taus)]
-
-    @pl.when(late_above1)
-    def _():
-        heard(0)
-        tails_copy.start()
-        halo_copy.start()
-
-    pl.when(late_above2)(lambda: heard(1))
+    def inner_frames():
+        own = vv[...]
+        turned = pltpu.roll(own, rows - WIDTH, 1)
+        frames = []
+        for k in range(chains - 1):
+            lo = WIDTH * k
+            v = own[:, lo : lo + LANES] if k % 2 == 0 else turned[:, lo - WIDTH : lo - WIDTH + LANES]
+            frames.append(jnp.where(window, v, 0.0))
+        return frames, [2.0 / jnp.sum(v * v, axis=1, keepdims=True) for v in frames]
+
+    def upper_frame():
+        v = jnp.concatenate([vv[:, rows - WIDTH : rows], heads[:, 0:WIDTH]], axis=1)
+        v = jnp.where(window & ((lane_of < WIDTH) | has_above1), v, 0.0)
+        return v, 2.0 / jnp.sum(v * v, axis=1, keepdims=True)
+
+    def keep(products):
+        single[...] = products[chains - 2][0:FRAME]
+        for i, k in enumerate(range(chains - 3, 0, -2)):
+            pairs[i] = paired(products[k], products[k - 1])
+
+    def run_upper(product):
+        raw = xe[top : top + WIDTH, :]
+        upper[...] = raw - dot(product[0:WIDTH, 0:FRAME], jnp.concatenate([raw, rim], axis=0))
+
+    top = rows
+    x_copy.wait()
+
+    prompt = lax.rem(b, 2) == 0
+
+    @pl.when(prompt)
+    def _():
+        pl.when(has_above1)(heads_copy.wait_recv)
+        frames, taus = inner_frames()
+        v, tau = upper_frame()
+        products = [product for _, product in combined(frames + [v], taus + [tau])]
+        keep(products)
+        run_upper(products[chains - 1])
+
+    @pl.when(jnp.logical_not(prompt))
+    def _():
+        keep([product for _, product in combined(*inner_frames())])
 
     @pl.when(next_below1)
     def _():
         heard(2)
         heads_copy.start()
 
-    x_copy.wait()
-    form = unit - products[0][0:RIM]
-    outflow = dot(form[:, 0:WIDTH], xe[WIDTH : 2 * WIDTH, 0:cols])
-    for k in range(1, chains - 1):
-        form = dot(form[:, WIDTH:FRAME], unit - products[k][0:RIM])
-        outflow = outflow + dot(form[:, 0:WIDTH], xe[WIDTH * (k + 1) : WIDTH * (k + 2), 0:cols])
-    onward = form[:, WIDTH:FRAME]
-
-    fsend[...] = outflow[0:EARLY] + dot(onward[0:EARLY], xe[rows : rows + RIM, 0:cols])
-    pl.when(next_below2)(lambda: heard(3))
-    pl.when(soon_below2 | next_below2)(far_copy.start)
-
-    pl.when(has_above1)(heads_copy.wait_recv)
-    v = jnp.concatenate([own[:, rows - WIDTH : rows], heads[:, 0:WIDTH]], axis=1)
-    v = jnp.where(window & ((lane_of < WIDTH) | has_above1), v, 0.0)
-    tau = 2.0 / jnp.sum(v * v, axis=1, keepdims=True)
-    ((_, product),) = combined([v], [tau])
-    products.append(product)
-    form = dot(onward, unit - product[0:RIM])
-    osend[:, 0:cols] = outflow + dot(form[:, 0:WIDTH], xe[rows : rows + WIDTH, 0:cols])
-    osend[:, cols:wide] = jnp.concatenate([form[:, WIDTH:LANES], jnp.zeros((RIM, WIDTH), F32)], axis=1)
-
+    frame = jnp.concatenate([xe[top - WIDTH : top, :], rim], axis=0)
+    frame = frame - dot(single[:, 0:FRAME], frame)
+    xe[top - WIDTH : top, :] = frame[0:WIDTH]
+    above = frame[WIDTH:FRAME]
+    span = WIDTH + FRAME
+    for i, k in enumerate(range(chains - 3, 0, -2)):
+        lo = WIDTH * k
+        frame = xe[lo : lo + span, :]
+        xe[lo : lo + span, :] = frame - dot(pairs[i], frame)
+
+    def send_far():
+        pl.when(next_below2)(lambda: heard(3))
+        pl.when(soon_below2 | next_below2)(far_copy.start)
+
+    fsend[...] = xe[WIDTH : WIDTH + EARLY, 0:cols] + dot(
+        xe[WIDTH : WIDTH + EARLY, cols : cols + RIM], xe[top : top + RIM, 0:cols]
+    )
+
+    send_far()
+
+    @pl.when(jnp.logical_not(prompt))
+    def _():
+        pl.when(slow_above1)(send_up)
+        pl.when(has_above1)(heads_copy.wait_recv)
+        v, tau = upper_frame()
+        ((_, product),) = combined([v], [tau])
+        run_upper(product)
+
+    flow = jnp.concatenate(
+        [xe[WIDTH : WIDTH + RIM, 0:cols], jnp.zeros((RIM, LANES), F32)], axis=1
+    ) + dot(xe[WIDTH : WIDTH + RIM, cols : cols + RIM], upper[0:RIM, :])
+    osend[...] = flow
     pl.when(soon_below1 | next_below1)(near_copy.start)
+
+    carried = jnp.concatenate([xe[WIDTH + RIM : top, :], above], axis=0)
+    xe[WIDTH : WIDTH + RIM, :] = flow
+    moved = dot(carried[:, cols : cols + RIM], upper[0:RIM, :])
+    xe[WIDTH + RIM : top + RIM, 0:cols] = carried[:, 0:cols] + moved[:, 0:cols]
+    xe[WIDTH + RIM : top + RIM, cols:wide] = moved[:, cols:wide]
+    xe[top + RIM : top + WIDTH, :] = upper[RIM:WIDTH, :]
 
     def lower_chain():
         pl.when(has_below1 & jnp.logical_not(last_below1))(tails_copy.wait_recv)
@@ -290,12 +351,19 @@
         first_product[...] = product[WIDTH:FRAME]
 
 
-    for k in range(chains - 1, -1, -1):
-        lo = WIDTH * (k + 1)
-        frame = xe[lo : lo + FRAME, :]
-        xe[lo : lo + FRAME, :] = frame - dot(products[k][0:FRAME, 0:FRAME], frame)
-
-    pl.when(jnp.logical_not(lower_last))(lower_chain)
+    @pl.when(jnp.logical_not(lower_last))
+    def _():
+        lower_chain()
+        pl.when(has_below1)(halo_copy.wait_recv)
+        xe[WIDTH : WIDTH + RIM, :] = xe[WIDTH : WIDTH + RIM, :] - dot(
+            first_product[:, 0:FRAME], xe[0:FRAME, :]
+        )
+
+    answer = xe[WIDTH : WIDTH + rows, cols:wide]
+    head = answer.astype(jnp.bfloat16).astype(F32)
+    reply[...] = (
+        head + pltpu.roll(head, SLOT, 1) + pltpu.roll(answer - head, 2 * SLOT, 1)
+    ).astype(jnp.bfloat16)
 
     @pl.when(last_below1)
     def _():
@@ -318,14 +386,19 @@
         ],
         axis=0,
     )
-    y_ref[...] = xe[WIDTH : WIDTH + rows, 0:cols] + dot(
-        xe[WIDTH : WIDTH + rows, cols : cols + RIM], inflow
-    )
-
-    pl.when(lower_last)(lower_chain)
-    pl.when(has_below1)(halo_copy.wait_recv)
-    frame = jnp.concatenate([xe[0:WIDTH, 0:cols], y_ref[0:RIM, :]], axis=0)
-    y_ref[0:RIM, :] = y_ref[0:RIM, :] - dot(first_product[:, 0:FRAME], frame)
+    head = inflow.astype(jnp.bfloat16).astype(F32)
+    gap = jnp.zeros((SLOT - RIM, cols), F32)
+    stack = jnp.concatenate([head, gap, inflow - head, gap, head, gap, jnp.zeros((SLOT, cols), F32)], axis=0)
+    y_ref[...] = xe[WIDTH : WIDTH + rows, 0:cols] + jnp.dot(
+        reply[...], stack.astype(jnp.bfloat16), preferred_element_type=F32
+    )
+
+    @pl.when(lower_last)
+    def _():
+        lower_chain()
+        pl.when(has_below1)(halo_copy.wait_recv)
+        frame = jnp.concatenate([xe[0:WIDTH, 0:cols], y_ref[0:RIM, :]], axis=0)
+        y_ref[0:RIM, :] = y_ref[0:RIM, :] - dot(first_product[:, 0:FRAME], frame)
 
     for copy in gathers:
         copy.wait_send()
@@ -357,7 +430,7 @@
         out_specs=pl.BlockSpec(memory_space=pltpu.VMEM),
         scratch_shapes=[
             pltpu.SMEM((SWEEPS,), jnp.int32),
-            pltpu.VMEM((WIDTH + rows + RIM, wide), F32),
+            pltpu.VMEM((WIDTH + rows, wide), F32),
             pltpu.VMEM((col_count, per, rows), F32),
             pltpu.VMEM((SWEEPS, rows), F32),
             pltpu.VMEM((SWEEPS, LANES), F32),
@@ -368,6 +441,10 @@
             pltpu.VMEM((RIM, wide), F32),
             pltpu.VMEM((EARLY, cols), F32),
             pltpu.VMEM((RIM, LANES), F32),
+            pltpu.VMEM((WIDTH, wide), F32),
+            pltpu.VMEM((FRAME, LANES), F32),
+            pltpu.VMEM(((rows // WIDTH - 2) // 2, WIDTH + FRAME, WIDTH + FRAME), F32),
+            pltpu.VMEM((rows, LANES), jnp.bfloat16),
             pltpu.SemaphoreType.DMA((3,)),
             pltpu.SemaphoreType.DMA((col_count,)),
             pltpu.SemaphoreType.DMA((col_count,)),

time: 20.5 us -> 20 us (0.976)
  Pallas kernels: 19.4 us -> 18.9 us
    pallas_call x1, Pallas kernels: 19.4 us -> 18.9 us  [local(): pl.pallas_call(functools.partial(sweep_kernel, row_count, col_count), out...]
where the time goes in v5:
time: 20 us; the launch traced here: 19.9 us
  Pallas kernels  18.9 us (94%)
  local copies, waits for them, and re-layouts  0.97 us (5%)
    pallas_call x1, Pallas kernels, local(): pl.pallas_call(functools.partial(sweep_kernel, row_count, col_count), out...  18.9 us
    unnamed x1, local copies, waits for them, and re-layouts  0.97 us

profile of v5, /device:TPU:1, one launch (start us, length us, event | category | flops | bytes accessed | tf_op | source)
XLA Modules:
  0.0 19.9 jit_solution(7119010083142221206)
XLA Ops:
  0.0 18.9 %sweep.1 = f32[512,512]{1,0:T(8,128)S(1)} custom-call(s32[16]{0:T(128)} %off_hbm.1, f32[2,512]{1,0:T(2,128)} %refl_hbm.1, f32[512,512]{1,0:T(8,128)} %x_hbm.1), custom_call_target="tpu_custom_call" | custom-call | tf_op jit(solution)/shard_map/sweep/pallas_call | solution.py:426
  18.9 1.0 %copy.5 = f32[512,512]{1,0:T(8,128)} copy(f32[512,512]{1,0:T(8,128)S(1)} %sweep.1) | data formatting | bytes 2097152

commit v6 on v5

--- a/solution.py
+++ b/solution.py
@@ -50,7 +50,7 @@
     tau = jnp.concatenate(taus, axis=0)
     n = v_all.shape[0]
     gram = lax.dot_general(
-        v_all, v_all, (((1,), (1,)), ((), ())), precision=HIGHEST, preferred_element_type=F32
+        v_all, v_all, (((1,), (1,)), ((), ())), precision=HIGH, preferred_element_type=F32
     )
     scaled = gram * tau
     w_all = v_all * tau
@@ -90,7 +90,7 @@
     off_hbm, refl_hbm, x_hbm,
     y_ref,
     off_ref, xe, vrec, vv, heads, tails, tv, osend, fsend, orec, o2rec, first_product, upper, single, pairs, reply,
-    local_sems, send_sems, recv_sems, tail_send, tail_recv, edge_send, edge_recv, ready,
+    local_sems, send_sems, recv_sems, tail_send, tail_recv, edge_send, edge_recv, ready, answered,
 ):
     per, rows = refl_hbm.shape
     cols = x_hbm.shape[1]
@@ -111,7 +111,7 @@
     soon_above1, soon_above2 = has_above1 & jnp.logical_not(late_above1), has_above2 & jnp.logical_not(late_above2)
     last_below1, last_below2 = late_below1 & (place == 0), late_below2 & (place < 2)
     next_below1, next_below2 = late_below1 & (place > 0), late_below2 & (place > 1)
-    lower_last = (place == 0) | (b == 1)
+    lower_last = place == 0
     wide_above1 = soon_above1 & (place == TURN - 1)
     neighbours = (
         (above1, late_above1, soon_above1, 0),
@@ -129,8 +129,26 @@
         return lax.rem(c + d, col_count)
 
     order = sorted(range(1, col_count), key=lambda d: -min(d, col_count - d))
-    for d in order:
-        greet((b, col_at(d)))
+
+    def turn_of(col):
+        return jnp.where(2 * col <= col_count, 2 * col, 2 * (col_count - col) + 3)
+
+    by_turn = sorted(range(col_count), key=lambda p: 2 * p if 2 * p <= col_count else 2 * (col_count - p) + 3)
+    turn = turn_of(c)
+
+    def distance(p):
+        return lax.rem(p - c + col_count, col_count)
+
+    @pl.when(wide_above1)
+    def _():
+        for p in by_turn:
+            pl.when(turn_of(p) > turn)(functools.partial(greet, (b, p)))
+
+    @pl.when(jnp.logical_not(wide_above1))
+    def _():
+        for d in order:
+            greet((b, col_at(d)))
+
     for i, (peer, late, _, _) in enumerate(neighbours):
         if i == 2:
             late = next_below1
@@ -166,7 +184,10 @@
     def _():
         o2rec[...] = jnp.zeros((EARLY, cols), F32)
 
-    greeted = jnp.where(wide_above1, 2 * (col_count - 1), col_count - 1)
+    sooner = 0
+    for p in by_turn:
+        sooner = sooner + (turn_of(p) < turn).astype(jnp.int32)
+    greeted = jnp.where(wide_above1, sooner + col_count - 1, col_count - 1)
     for _, _, soon, _ in neighbours:
         greeted = greeted + soon.astype(jnp.int32)
     pl.semaphore_wait(barrier, greeted)
@@ -179,8 +200,33 @@
         )
         for d in order
     ]
-    for copy in gathers:
-        copy.start()
+
+    def gather_to(p):
+        return pltpu.make_async_remote_copy(
+            src_ref=vrec.at[c], dst_ref=vrec.at[c],
+            send_sem=send_sems.at[distance(p)], recv_sem=recv_sems.at[distance(p)],
+            device_id=(b, p), device_id_type=MESH,
+        )
+
+    def answer(p):
+        gather_to(p).start()
+        pl.semaphore_signal(
+            answered.at[col_count - distance(p)], inc=1, device_id=(b, p), device_id_type=MESH
+        )
+
+    def follow(p):
+        pl.semaphore_wait(answered.at[distance(p)], 1)
+        gather_to(p).start()
+
+    @pl.when(wide_above1)
+    def _():
+        for p in by_turn:
+            pl.when(turn_of(p) < turn)(functools.partial(answer, p))
+
+    @pl.when(jnp.logical_not(wide_above1))
+    def _():
+        for copy in gathers:
+            copy.start()
 
     def edge(i, src, dst, peer):
         return pltpu.make_async_remote_copy(
@@ -199,7 +245,9 @@
         for d in range(col_count)
     ]
     heads_copy = edge(2, vv.at[:, 0:LANES], heads, below1)
-    near_copy = edge(3, osend, orec, below1)
+    near_copy = edge(3, osend.at[:, 0:cols], orec.at[:, 0:cols], below1)
+    early = RIM - EARLY
+    reply_copy = edge(5, osend.at[early:RIM, cols:wide], orec.at[early:RIM, cols:wide], below1)
     far_copy = edge(4, fsend, o2rec, below2)
 
     def tell(i, peer):
@@ -218,6 +266,11 @@
             copy.start()
 
     pl.when(soon_above1)(halo_copy.start)
+
+    @pl.when(wide_above1)
+    def _():
+        for p in by_turn:
+            pl.when(turn_of(p) > turn)(functools.partial(follow, p))
 
 
     off_copy.wait()
@@ -280,8 +333,8 @@
         frames, taus = inner_frames()
         v, tau = upper_frame()
         products = [product for _, product in combined(frames + [v], taus + [tau])]
+        run_upper(products[chains - 1])
         keep(products)
-        run_upper(products[chains - 1])
 
     @pl.when(jnp.logical_not(prompt))
     def _():
@@ -306,28 +359,45 @@
         pl.when(next_below2)(lambda: heard(3))
         pl.when(soon_below2 | next_below2)(far_copy.start)
 
-    fsend[...] = xe[WIDTH : WIDTH + EARLY, 0:cols] + dot(
-        xe[WIDTH : WIDTH + EARLY, cols : cols + RIM], xe[top : top + RIM, 0:cols]
-    )
-
-    send_far()
+    def set_far():
+        fsend[...] = xe[WIDTH : WIDTH + EARLY, 0:cols] + dot(
+            xe[WIDTH : WIDTH + EARLY, cols : cols + RIM], xe[top : top + RIM, 0:cols]
+        )
+
+    def set_near():
+        flow = jnp.concatenate(
+            [xe[WIDTH : WIDTH + RIM, 0:cols], jnp.zeros((RIM, LANES), F32)], axis=1
+        ) + dot(xe[WIDTH : WIDTH + RIM, cols : cols + RIM], upper[0:RIM, :])
+        osend[...] = flow
+
+    near_now = soon_below1 | next_below1
+
+    @pl.when(prompt)
+    def _():
+        set_far()
+        set_near()
+        pl.when(near_now)(reply_copy.start)
+        send_far()
+        pl.when(near_now)(near_copy.start)
 
     @pl.when(jnp.logical_not(prompt))
     def _():
+        set_far()
+        send_far()
         pl.when(slow_above1)(send_up)
         pl.when(has_above1)(heads_copy.wait_recv)
         v, tau = upper_frame()
         ((_, product),) = combined([v], [tau])
         run_upper(product)
-
-    flow = jnp.concatenate(
-        [xe[WIDTH : WIDTH + RIM, 0:cols], jnp.zeros((RIM, LANES), F32)], axis=1
-    ) + dot(xe[WIDTH : WIDTH + RIM, cols : cols + RIM], upper[0:RIM, :])
-    osend[...] = flow
-    pl.when(soon_below1 | next_below1)(near_copy.start)
+        set_near()
+
+        @pl.when(near_now)
+        def _():
+            reply_copy.start()
+            near_copy.start()
 
     carried = jnp.concatenate([xe[WIDTH + RIM : top, :], above], axis=0)
-    xe[WIDTH : WIDTH + RIM, :] = flow
+    xe[WIDTH : WIDTH + RIM, :] = osend[...]
     moved = dot(carried[:, cols : cols + RIM], upper[0:RIM, :])
     xe[WIDTH + RIM : top + RIM, 0:cols] = carried[:, 0:cols] + moved[:, 0:cols]
     xe[WIDTH + RIM : top + RIM, cols:wide] = moved[:, cols:wide]
@@ -369,6 +439,7 @@
     def _():
         heard(2)
         heads_copy.start()
+        reply_copy.start()
         near_copy.start()
 
     @pl.when(last_below2)
@@ -376,15 +447,12 @@
         heard(3)
         far_copy.start()
 
+    pl.when(has_above1)(reply_copy.wait_recv)
+    pl.when(has_above2)(far_copy.wait_recv)
+    passed = dot(orec[early:RIM, cols : cols + EARLY], o2rec[...])
     pl.when(has_above1)(near_copy.wait_recv)
-    pl.when(has_above2)(far_copy.wait_recv)
-    early = RIM - EARLY
     inflow = jnp.concatenate(
-        [
-            orec[0:early, 0:cols],
-            orec[early:RIM, 0:cols] + dot(orec[early:RIM, cols : cols + EARLY], o2rec[...]),
-        ],
-        axis=0,
+        [orec[0:early, 0:cols], orec[early:RIM, 0:cols] + passed], axis=0
     )
     head = inflow.astype(jnp.bfloat16).astype(F32)
     gap = jnp.zeros((SLOT - RIM, cols), F32)
@@ -414,6 +482,7 @@
     @pl.when(has_below1)
     def _():
         heads_copy.wait_send()
+        reply_copy.wait_send()
         near_copy.wait_send()
 
     pl.when(has_below2)(far_copy.wait_send)
@@ -450,9 +519,10 @@
             pltpu.SemaphoreType.DMA((col_count,)),
             pltpu.SemaphoreType.DMA((col_count,)),
             pltpu.SemaphoreType.DMA((col_count,)),
-            pltpu.SemaphoreType.DMA((5,)),
-            pltpu.SemaphoreType.DMA((5,)),
+            pltpu.SemaphoreType.DMA((6,)),
+            pltpu.SemaphoreType.DMA((6,)),
             pltpu.SemaphoreType.REGULAR((4,)),
+            pltpu.SemaphoreType.REGULAR((col_count,)),
         ],
         compiler_params=pltpu.CompilerParams(
             collective_id=0, has_side_effects=True, vmem_limit_bytes=24 * 2**20

time: 20 us -> 19.5 us (0.975)
  the two profiles are of different devices: /device:TPU:1 before, /device:TPU:195 now
where the time goes in v6:
time: 19.5 us; the launch traced here: 19.4 us
  Pallas kernels  18.4 us (94%)
  local copies, waits for them, and re-layouts  0.97 us (5%)
    pallas_call x1, Pallas kernels, local(): pl.pallas_call(functools.partial(sweep_kernel, row_count, col_count), out...  18.4 us
    unnamed x1, local copies, waits for them, and re-layouts  0.97 us

profile of v6, /device:TPU:195, one launch (start us, length us, event | category | flops | bytes accessed | tf_op | source)
XLA Modules:
  0.0 19.4 jit_solution(12313194346371511907)
XLA Ops:
  0.0 18.4 %sweep.1 = f32[512,512]{1,0:T(8,128)S(1)} custom-call(s32[16]{0:T(128)} %off_hbm.1, f32[2,512]{1,0:T(2,128)} %refl_hbm.1, f32[512,512]{1,0:T(8,128)} %x_hbm.1), custom_call_target="tpu_custom_call" | custom-call | tf_op jit(solution)/shard_map/sweep/pallas_call | solution.py:495
  18.4 1.0 %copy.5 = f32[512,512]{1,0:T(8,128)} copy(f32[512,512]{1,0:T(8,128)S(1)} %sweep.1) | data formatting | bytes 2097152

commit v7 on v6

--- a/solution.py
+++ b/solution.py
@@ -332,7 +332,9 @@
         pl.when(has_above1)(heads_copy.wait_recv)
         frames, taus = inner_frames()
         v, tau = upper_frame()
-        products = [product for _, product in combined(frames + [v], taus + [tau])]
+        frames, taus = frames + [v], taus + [tau]
+        half = chains // 2
+        products = [p for _, p in combined(frames[:half], taus[:half]) + combined(frames[half:], taus[half:])]
         run_upper(products[chains - 1])
         keep(products)
 

time: 19.5 us -> 19.5 us (level)
  the two profiles are of different devices: /device:TPU:195 before, /device:TPU:197 now
where the time goes in v7:
time: 19.5 us; the launch traced here: 19.4 us
  Pallas kernels  18.4 us (94%)
  local copies, waits for them, and re-layouts  0.97 us (5%)
    pallas_call x1, Pallas kernels, local(): pl.pallas_call(functools.partial(sweep_kernel, row_count, col_count), out...  18.4 us
    unnamed x1, local copies, waits for them, and re-layouts  0.97 us

profile of v7, /device:TPU:197, one launch (start us, length us, event | category | flops | bytes accessed | tf_op | source)
XLA Modules:
  0.0 19.4 jit_solution(1987028019722801732)
XLA Ops:
  0.0 18.4 %sweep.1 = f32[512,512]{1,0:T(8,128)S(1)} custom-call(s32[16]{0:T(128)} %off_hbm.1, f32[2,512]{1,0:T(2,128)} %refl_hbm.1, f32[512,512]{1,0:T(8,128)} %x_hbm.1), custom_call_target="tpu_custom_call" | custom-call | tf_op jit(solution)/shard_map/sweep/pallas_call | solution.py:497
  18.4 1.0 %copy.5 = f32[512,512]{1,0:T(8,128)} copy(f32[512,512]{1,0:T(8,128)S(1)} %sweep.1) | data formatting | bytes 2097152

commit v8 on v7

--- a/solution.py
+++ b/solution.py
@@ -28,6 +28,11 @@
 def halves(x):
     head = x.astype(jnp.bfloat16)
     return head, (x - head.astype(F32)).astype(jnp.bfloat16)
+
+
+def scaled_rows(v, dead=0.0):
+    v = v * lax.rsqrt(jnp.sum(v * v, axis=1, keepdims=True) + dead)
+    return v, 2.0 / (jnp.sum(v * v, axis=1, keepdims=True) + dead)
 
 
 def substituted(scaled, base, w):
@@ -305,13 +310,13 @@
         for k in range(chains - 1):
             lo = WIDTH * k
             v = own[:, lo : lo + LANES] if k % 2 == 0 else turned[:, lo - WIDTH : lo - WIDTH + LANES]
-            frames.append(jnp.where(window, v, 0.0))
-        return frames, [2.0 / jnp.sum(v * v, axis=1, keepdims=True) for v in frames]
+            frames.append(scaled_rows(jnp.where(window, v, 0.0)))
+        return [v for v, _ in frames], [tau for _, tau in frames]
 
     def upper_frame():
         v = jnp.concatenate([vv[:, rows - WIDTH : rows], heads[:, 0:WIDTH]], axis=1)
         v = jnp.where(window & ((lane_of < WIDTH) | has_above1), v, 0.0)
-        return v, 2.0 / jnp.sum(v * v, axis=1, keepdims=True)
+        return scaled_rows(v)
 
     def keep(products):
         single[...] = products[chains - 2][0:FRAME]
@@ -418,7 +423,8 @@
         v = jnp.concatenate([tv[:, WIDTH:LANES], vv[:, 0:WIDTH]], axis=1)
         v = jnp.where(window & has_below1, v, 0.0)
         dead = jnp.where(has_below1, 0.0, 1.0)
-        tau = jnp.where(has_below1, 2.0 / (jnp.sum(v * v, axis=1, keepdims=True) + dead), 0.0)
+        v, tau = scaled_rows(v, dead)
+        tau = jnp.where(has_below1, tau, 0.0)
         ((_, product),) = combined([v], [tau])
         first_product[...] = product[WIDTH:FRAME]
 

time: 19.5 us -> 19.7 us (1.010)
  no operation moved by 1% of the time
where the time goes in v8:
time: 19.7 us; the launch traced here: 19.5 us
  Pallas kernels  18.5 us (94%)
  local copies, waits for them, and re-layouts  0.97 us (5%)
    pallas_call x1, Pallas kernels, local(): pl.pallas_call(functools.partial(sweep_kernel, row_count, col_count), out...  18.5 us
    unnamed x1, local copies, waits for them, and re-layouts  0.97 us

profile of v8, /device:TPU:197, one launch (start us, length us, event | category | flops | bytes accessed | tf_op | source)
XLA Modules:
  0.0 19.5 jit_solution(17639980556182615470)
XLA Ops:
  0.0 18.5 %sweep.1 = f32[512,512]{1,0:T(8,128)S(1)} custom-call(s32[16]{0:T(128)} %off_hbm.1, f32[2,512]{1,0:T(2,128)} %refl_hbm.1, f32[512,512]{1,0:T(8,128)} %x_hbm.1), custom_call_target="tpu_custom_call" | custom-call | tf_op jit(solution)/shard_map/sweep/pallas_call | solution.py:503
  18.5 1.0 %copy.5 = f32[512,512]{1,0:T(8,128)} copy(f32[512,512]{1,0:T(8,128)S(1)} %sweep.1) | data formatting | bytes 2097152

commit v9 on v8

--- a/solution.py
+++ b/solution.py
@@ -31,8 +31,9 @@
 
 
 def scaled_rows(v, dead=0.0):
-    v = v * lax.rsqrt(jnp.sum(v * v, axis=1, keepdims=True) + dead)
-    return v, 2.0 / (jnp.sum(v * v, axis=1, keepdims=True) + dead)
+    squares = jnp.sum(v * v, axis=1, keepdims=True) + dead
+    scale = lax.rsqrt(squares)
+    return v * scale, 2.0 / (squares * scale * scale)
 
 
 def substituted(scaled, base, w):

time: 19.7 us -> 19.6 us (level)
  no operation moved by 1% of the time
where the time goes in v9:
time: 19.6 us; the launch traced here: 19.5 us
  Pallas kernels  18.5 us (94%)
  local copies, waits for them, and re-layouts  0.97 us (5%)
    pallas_call x1, Pallas kernels, local(): pl.pallas_call(functools.partial(sweep_kernel, row_count, col_count), out...  18.5 us
    unnamed x1, local copies, waits for them, and re-layouts  0.97 us

profile of v9, /device:TPU:197, one launch (start us, length us, event | category | flops | bytes accessed | tf_op | source)
XLA Modules:
  0.0 19.5 jit_solution(8429257906594008039)
XLA Ops:
  0.0 18.5 %sweep.1 = f32[512,512]{1,0:T(8,128)S(1)} custom-call(s32[16]{0:T(128)} %off_hbm.1, f32[2,512]{1,0:T(2,128)} %refl_hbm.1, f32[512,512]{1,0:T(8,128)} %x_hbm.1), custom_call_target="tpu_custom_call" | custom-call | tf_op jit(solution)/shard_map/sweep/pallas_call | solution.py:504
  18.5 1.0 %copy.5 = f32[512,512]{1,0:T(8,128)} copy(f32[512,512]{1,0:T(8,128)S(1)} %sweep.1) | data formatting | bytes 2097152
